TPU v7x, 256 devices: a whole 4x4x8 slice. The times are simulated.
256 devices in a mesh: dp: 8 (over y, core), lang: 32 (over x, z).
Axes of the slice: x: 4, y: 4, z: 8, core: 2. Of those that a mesh axis runs over, the one named last changes fastest.
Arguments:
- inputs: bfloat16 [32768, 2048], P(('dp', 'lang')), may hold values from -6 to 6
- grad_out: bfloat16 [32768, 2048], P(('dp', 'lang')), may hold values from -6 to 6
- lang_ids: int32 [32768], P(('dp', 'lang')), may hold values from 0 to 199, as said below
- lang_block: int32 [200], replicated, may hold values from 0 to 31, as said below
- block_owner: int32 [32], replicated, may hold values from 0 to 31, each once
- w_in: bfloat16 [32, 4096, 2048], P('lang', 'dp'), may hold values from -0.125 to 0.125
- w_out: bfloat16 [32, 4096, 2048], P('lang', 'dp'), may hold values from -0.09375 to 0.09375
Outputs:
- grad_in: bfloat16 [32768, 2048], P(('dp', 'lang'))
- grad_w_in: bfloat16 [32, 4096, 2048], P('lang', 'dp')
- grad_w_out: bfloat16 [32, 4096, 2048], P('lang', 'dp')
Inputs may be any that keep to these rules, and one draw needn't show every extreme that they name: `lang_ids`: through lang_block, the 128 rows of one device name any one block at most 5 times; in every draw one block is named exactly 5 times by the rows of every device. `lang_block`: every block has at least one language. A permutation: block b's weights and gradients sit at index block_owner[b] of the block dimension.
All inputs are finite; a program needn't handle non-finite values.
Results may differ from a plain program's by a relative error of at most 0.019.
Values may be sent and summed in bfloat16 or wider, within the bound.
A program may use at most 128 MiB of HBM per device.

v0:
```python
import math

import jax
import jax.numpy as jnp
from jax import lax
from jax.sharding import PartitionSpec as P

gelu_scale = math.sqrt(2.0 / math.pi)


def gelu_parts(pre_act):
    tanh_arg = gelu_scale * (pre_act + 0.044715 * pre_act * pre_act * pre_act)
    tangent = jnp.tanh(tanh_arg)
    gelu_value = 0.5 * pre_act * (1.0 + tangent)
    gelu_slope = 0.5 * (1.0 + tangent) + 0.5 * pre_act * (1.0 - tangent * tangent) * gelu_scale * (
        1.0 + 3.0 * 0.044715 * pre_act * pre_act
    )
    return (gelu_value, gelu_slope)


def local_grads(gathered, w_first, w_second):
    rows_x = gathered[:, 0]
    rows_g = gathered[:, 1]
    pre_act = jnp.dot(rows_x, w_first.T, preferred_element_type=jnp.float32)
    gelu_value, gelu_slope = gelu_parts(pre_act)
    activated = gelu_value.astype(jnp.bfloat16)
    back_grad = jnp.dot(rows_g, w_second.T, preferred_element_type=jnp.float32)
    pre_grad = (back_grad * gelu_slope).astype(jnp.bfloat16)
    g_out = jnp.dot(activated.T, rows_g, preferred_element_type=jnp.float32).astype(jnp.bfloat16)
    g_in = jnp.dot(pre_grad.T, rows_x, preferred_element_type=jnp.float32).astype(jnp.bfloat16)
    return (pre_grad, g_in, g_out)


def body(inputs, grad_out, lang_ids, lang_block, block_owner, w_in, w_out):
    tok_rows = inputs.shape[0]
    feat_width = inputs.shape[1]
    lang_count = lax.axis_size("lang")
    dp_count = lax.axis_size("dp")
    per_peer = 5 * tok_rows // (4 * lang_count)
    languages = lang_block.shape[0]
    block_count = block_owner.shape[0]
    lang_hits = (lang_ids[:, None] == jnp.arange(languages, dtype=jnp.int32)[None, :]).astype(
        jnp.int32
    )
    row_block = jnp.sum(lang_hits * lang_block[None, :], axis=1)
    block_hits = (row_block[:, None] == jnp.arange(block_count, dtype=jnp.int32)[None, :]).astype(
        jnp.int32
    )
    holder = jnp.sum(block_hits * block_owner[None, :], axis=1)
    holder_hits = (holder[:, None] == jnp.arange(lang_count, dtype=jnp.int32)[None, :]).astype(
        jnp.int32
    )
    earlier = jnp.cumsum(holder_hits, axis=0) - holder_hits
    slot_index = jnp.sum(earlier * holder_hits, axis=1)
    position = holder * per_peer + slot_index
    packed = jnp.stack([inputs, grad_out], axis=1)
    w_first = w_in[0]
    w_second = w_out[0]
    col_rows, col_pos = (
        lax.all_gather(packed[None], "dp", axis=0, tiled=True),
        lax.all_gather(position[None], "dp", axis=0, tiled=True),
    )
    dp_index = jnp.arange(dp_count, dtype=jnp.int32)[:, None]
    target = col_pos // per_peer * (dp_count * per_peer) + dp_index * per_peer + col_pos % per_peer
    outgoing = jnp.zeros((lang_count * dp_count * per_peer, 2, feat_width), jnp.bfloat16)
    outgoing = outgoing.at[target.reshape(-1)].set(col_rows.reshape(-1, 2, feat_width), mode="drop")
    arrived = lax.all_to_all(
        outgoing.reshape(lang_count, dp_count * per_peer, 2, feat_width),
        "lang",
        split_axis=0,
        concat_axis=0,
        tiled=True,
    )
    gathered = arrived.reshape(-1, 2, feat_width)
    pre_grad, g_in, g_out = local_grads(gathered, w_first, w_second)
    partial_dx = jnp.dot(pre_grad, w_first, preferred_element_type=jnp.float32)
    partial_dx = partial_dx.reshape(lang_count, dp_count, per_peer, feat_width)
    summed = (
        lax.psum_scatter(partial_dx.astype(jnp.bfloat16), "dp", scatter_dimension=1, tiled=True)
        .astype(jnp.float32)
        .reshape(lang_count, per_peer, feat_width)
    )
    returned = lax.all_to_all(
        summed.astype(jnp.bfloat16), "lang", split_axis=0, concat_axis=0, tiled=True
    )
    grad_in = returned.reshape(lang_count * per_peer, feat_width)[position]
    return (grad_in, g_in[None], g_out[None])


def solution(mesh):
    in_specs = (
        P(("dp", "lang"), None),
        P(("dp", "lang"), None),
        P(("dp", "lang")),
        P(),
        P(),
        P("lang", "dp", None),
        P("lang", "dp", None),
    )
    out_specs = (P(("dp", "lang"), None), P("lang", "dp", None), P("lang", "dp", None))
    return jax.shard_map(body, mesh=mesh, in_specs=in_specs, out_specs=out_specs, check_vma=False)
```

profile of v0, /device:TPU:32, one launch (start us, length us, event | category | flops | bytes accessed | tf_op | source)
XLA Modules:
  0.0 580.0 jit_solution(14757968906127118816)
XLA Ops:
  7.2 0.0 copy-start
  7.2 0.0 copy-start.2
  7.2 0.0 copy-start.3
  7.2 0.0 copy-start.5
  7.2 0.0 all-gather.5.cloned.1.call-start
  7.3 2.4 pad_maximum_fusion
  9.7 0.0 all-gather.5.cloned.1.call-update
  9.7 0.0 reduce-scatter.2.cloned.1.call-start
  9.7 0.0 copy-done.2
  9.7 0.0 copy-done.3
  9.8 0.1 select_reduce_fusion
  9.9 0.0 copy-done.5
  9.9 0.2 select_reduce_fusion.2
  10.0 0.1 fusion.23
  10.1 0.2 reduce_window_sum.11
  10.3 0.2 select_reduce_fusion.1
  10.5 10.8 %all-gather.2 = s32[8,1,128]{2,1,0:T(1,128)S(1)} all-gather(s32[1,1,128]{2,1,0:T(1,128)S(1)} %fusion.34), channel_id=2, replica_groups=mesh['dp'=8,'lang'=32] {'dp'}, dimensions={0}, use_global_device_ids=true | all-gather | bytes 4608 | tf_op jit(solution)/shard_map/all_gather | solution.py:61
  21.3 0.4 rem.15
  21.6 0.1 fusion.26
  21.7 43.7 %all-gather.5.cloned.1.call-done = bf16[1024,2,2048]{2,0,1:T(8,128)(2,1)} async-done(((bf16[128,2,2048]{2,0,1:T(8,128)(2,1)}), bf16[1024,2,2048]{2,0,1:T(8,128)(2,1)}) %all-gather.5.cloned.1.call-update) | async-done | bytes 8388624 | tf_op jit(solution)/shard_map/all_gather | solution.py:60
  65.4 16.4 %copy.33 = bf16[1024,2,2048]{2,1,0:T(2,128)(2,1)} copy(bf16[1024,2,2048]{2,0,1:T(8,128)(2,1)} %all-gather.5.cloned.1.call-done) | data formatting | bytes 16777216 | tf_op jit(solution)/shard_map/all_gather | solution.py:60
  81.8 6.6 %broadcast_in_dim.8 = bf16[1280,2,2048]{2,1,0:T(2,128)(2,1)} broadcast(bf16[]{:T(256)} %constant.15.clone.1), dimensions={} | broadcast | bytes 10485762 | tf_op jit(solution)/shard_map/broadcast_in_dim | solution.py:65
  88.4 127.9 %scatter_fusion = bf16[1280,2,2048]{2,1,0:T(2,128)(2,1)} fusion(bf16[1280,2,2048]{2,1,0:T(2,128)(2,1)} %broadcast_in_dim.8, s32[1024]{0:T(1024)S(1)} %bitcast.74, bf16[1024,2,2048]{2,1,0:T(2,128)(2,1)} %copy.33), kind=kCustom, calls=%fused_computation.1 | custom fusion | bytes 25169920 | tf_op jit(solution)/shard_map/scatter | solution.py:66
  216.3 241.2 %all_to_all.10 = bf16[32,40,2,2048]{3,2,1,0:T(2,128)(2,1)} all-to-all(bf16[32,40,2,2048]{3,2,1,0:T(2,128)(2,1)} %bitcast.62), channel_id=1, replica_groups=mesh['dp'=8,'lang'=32] {'lang'}, dimensions={0} | all-to-all | bytes 20971520 | tf_op jit(solution)/shard_map/all_to_all | solution.py:67
  457.5 12.9 %copy.34 = bf16[32,40,2,2048]{3,1,0,2:T(8,128)(2,1)} copy(bf16[32,40,2,2048]{3,2,1,0:T(2,128)(2,1)} %all_to_all.10) | data formatting | bytes 20971520 | tf_op jit(solution)/shard_map/all_to_all | solution.py:67
  470.4 0.0 copy-done
  470.4 0.0 copy-start.1
  470.4 0.0 copy-start.4
  470.4 5.2 fusion.3
  475.6 0.0 copy-start.6
  475.6 1.5 copy-done.6
  477.1 0.0 copy-done.1
  477.1 0.0 copy-done.4
  477.1 4.3 fusion.5
  481.4 1.6 dot_general.19
  483.0 4.9 convolution_convert_fusion
  487.9 5.2 copy.36
  493.1 0.0 reduce-scatter.2.cloned.1.call-update
  493.2 38.1 %reduce-scatter.2.cloned.1.call-done = bf16[32,1,5,2048]{3,0,2,1:T(8,128)(2,1)} async-done(((bf16[32,8,5,2048]{3,0,2,1:T(8,128)(2,1)}), bf16[32,1,5,2048]{3,0,2,1:T(8,128)(2,1)}) %reduce-scatter.2.cloned.1.call-update) | async-done | bytes 655376 | tf_op jit(solution)/shard_map/reduce_scatter | solution.py:79
  531.3 2.4 copy.37
  533.8 10.1 %all-to-all-start.1 = ((bf16[32,5,2048]{2,1,0:T(8,128)(2,1)}), bf16[32,5,2048]{2,1,0:T(8,128)(2,1)}, u32[]{:S(2)}, u32[]{:S(2)}) async-start(bf16[32,5,2048]{2,1,0:T(8,128)(2,1)} %copy.37), calls=%async_computation.2 | async-start | bytes 2097152 | tf_op jit(solution)/shard_map/all_to_all | solution.py:83
  543.9 0.0 copy-start.7
  543.9 6.7 %fusion.9 = bf16[1,512,2048]{2,1,0:T(8,128)(2,1)} fusion(bf16[1280,512]{1,0:T(8,128)(2,1)S(1)} %fusion.5, bf16[1280,2,2048]{2,0,1:T(8,128)(2,1)} %bitcast.64), kind=kOutput, calls=%fused_computation.16 | convolution fusion | flops 2685403136 | bytes 8650752 | tf_op jit(solution)/shard_map/dot_general | solution.py:30
  550.7 0.0 copy-done.7
  550.7 6.8 %fusion.8 = bf16[1,512,2048]{2,1,0:T(8,128)(2,1)} fusion(bf16[1280,2,2048]{2,0,1:T(8,128)(2,1)} %bitcast.65, f32[1280,512]{1,0:T(8,128)S(1)} %copy-done.7), kind=kOutput, calls=%fused_computation.15 | convolution fusion | flops 2691301376 | bytes 9961472 | tf_op jit(solution)/shard_map/dot_general | solution.py:29
  557.5 12.5 %all-to-all-done.1 = bf16[32,5,2048]{2,1,0:T(8,128)(2,1)} async-done(((bf16[32,5,2048]{2,1,0:T(8,128)(2,1)}), bf16[32,5,2048]{2,1,0:T(8,128)(2,1)}, u32[]{:S(2)}, u32[]{:S(2)}) %all-to-all-start.1) | async-done | bytes 655392 | tf_op jit(solution)/shard_map/all_to_all | solution.py:83
  570.0 1.5 reshape.110
  571.4 1.7 gather_fusion
  (6 shorter events, 0.0 us)
Async XLA Ops:
  7.2 463.2 %copy-start = (bf16[1,512,2048]{2,1,0:T(8,128)(2,1)S(1)}, bf16[1,512,2048]{2,1,0:T(8,128)(2,1)}, u32[]{:S(2)}) copy-start(bf16[1,512,2048]{2,1,0:T(8,128)(2,1)} %param.12) | copy-start | bytes 6291460
  7.2 2.6 copy-start.2
  7.2 2.6 copy-start.3
  7.2 2.7 copy-start.5
  7.2 58.2 %all-gather.5.cloned.1.call-start = ((), (), s32[]{:S(2)}) async-start(), calls=%async_computation.4 | async-start | bytes 9437184 | tf_op jit(solution)/shard_map/all_gather | solution.py:60
  9.7 521.6 %reduce-scatter.2.cloned.1.call-start = ((), (), s32[]{:S(2)}) async-start(), calls=%async_computation.3 | async-start | bytes 5898240 | tf_op jit(solution)/shard_map/reduce_scatter | solution.py:79
  470.4 6.7 %copy-start.1 = (bf16[32,40,2,2048]{3,1,0,2:T(8,128)(2,1)S(1)}, bf16[32,40,2,2048]{3,1,0,2:T(8,128)(2,1)}, u32[]{:S(2)}) copy-start(bf16[32,40,2,2048]{3,1,0,2:T(8,128)(2,1)} %copy.34) | copy-start | bytes 31457284
  470.4 6.7 %copy-start.4 = (bf16[1,512,2048]{2,1,0:T(8,128)(2,1)S(1)}, bf16[1,512,2048]{2,1,0:T(8,128)(2,1)}, u32[]{:S(2)}) copy-start(bf16[1,512,2048]{2,1,0:T(8,128)(2,1)} %param.13) | copy-start | bytes 6291460
  475.6 1.5 copy-start.6
  533.8 36.2 %all-to-all-start.1 = ((bf16[32,5,2048]{2,1,0:T(8,128)(2,1)}), bf16[32,5,2048]{2,1,0:T(8,128)(2,1)}, u32[]{:S(2)}, u32[]{:S(2)}) async-start(bf16[32,5,2048]{2,1,0:T(8,128)(2,1)} %copy.37), calls=%async_computation.2 | async-start | bytes 2097152 | tf_op jit(solution)/shard_map/all_to_all | solution.py:83
  543.9 6.8 %copy-start.7 = (f32[1280,512]{1,0:T(8,128)S(1)}, f32[1280,512]{1,0:T(8,128)}, u32[]{:S(2)}) copy-start(f32[1280,512]{1,0:T(8,128)} %copy-done.6) | copy-start | bytes 7864324
Sparse Core Ops, SparseCore 0:
  10.5 54.8 all-gather.4
  493.3 37.9 reduce-scatter.1
where the time goes:
time: 582 us; the launch traced here: 580 us
  blocking collectives  252 us (43%)
  local copies, waits for them, and re-layouts  178 us (31%)
  waiting for transfers between devices  94.3 us (16%)
  matrix products  28 us (5%)
  between operations  14.2 us (2%)
  starting transfers between devices  10.2 us (2%)
    all_to_all x1, blocking collectives, body(): lax.all_to_all(outgoing.reshape(lang_count, dp_count * per_peer, 2, feat_...  241 us
    scatter x1, local copies, waits for them, and re-layouts, body(): outgoing.at[target.reshape(-1)]  128 us
    all_gather x1, waiting for transfers between devices, body(): lax.all_gather(packed[None], 'dp', axis=0, tiled=True)  43.7 us
    reduce_scatter x1, waiting for transfers between devices, body(): lax.psum_scatter(partial_dx.astype(jnp.bfloat16), 'dp', scatter_dimension...  38.1 us
    all_gather x1, local copies, waits for them, and re-layouts, body(): lax.all_gather(packed[None], 'dp', axis=0, tiled=True)  16.4 us
    all_to_all x1, local copies, waits for them, and re-layouts, body(): lax.all_to_all(outgoing.reshape(lang_count, dp_count * per_peer, 2, feat_...  12.9 us
    all_to_all x1, waiting for transfers between devices, body(): lax.all_to_all(summed.astype(jnp.bfloat16), 'lang', split_axis=0, concat_...  12.5 us
  transfers between devices with their start and end apart: 3, of which 3 were waited for; matrix products, arithmetic and copies ran while one was open for 3% of the time, Pallas kernels for 0%

commit v1 on v0

v1 whole, which is shorter than its diff:
```python
import math

import jax
import jax.numpy as jnp
from jax import lax
from jax.sharding import PartitionSpec as P

gelu_scale = math.sqrt(2.0 / math.pi)
CAP = 5


def gelu_parts(pre_act):
    tanh_arg = gelu_scale * (pre_act + 0.044715 * pre_act * pre_act * pre_act)
    tangent = jnp.tanh(tanh_arg)
    gelu_value = 0.5 * pre_act * (1.0 + tangent)
    gelu_slope = 0.5 * (1.0 + tangent) + 0.5 * pre_act * (1.0 - tangent * tangent) * gelu_scale * (
        1.0 + 3.0 * 0.044715 * pre_act * pre_act
    )
    return (gelu_value, gelu_slope)


def local_grads(rows_x, rows_g, w_first, w_second):
    pre_act = jnp.dot(rows_x, w_first.T, preferred_element_type=jnp.float32)
    gelu_value, gelu_slope = gelu_parts(pre_act)
    activated = gelu_value.astype(jnp.bfloat16)
    back_grad = jnp.dot(rows_g, w_second.T, preferred_element_type=jnp.float32)
    pre_grad = (back_grad * gelu_slope).astype(jnp.bfloat16)
    g_out = jnp.dot(activated.T, rows_g, preferred_element_type=jnp.float32).astype(jnp.bfloat16)
    g_in = jnp.dot(pre_grad.T, rows_x, preferred_element_type=jnp.float32).astype(jnp.bfloat16)
    return (pre_grad, g_in, g_out)


def slots_of(lang_ids, lang_block, block_owner):
    rows = lang_ids.shape[0]
    holder_of_lang = jnp.sum(
        jnp.where(lang_block[:, None] == jnp.arange(block_owner.shape[0])[None, :], block_owner[None, :], 0), axis=1
    )
    holder = jnp.sum(
        jnp.where(lang_ids[:, None] == jnp.arange(lang_block.shape[0])[None, :], holder_of_lang[None, :], 0), axis=1
    )
    row = jnp.arange(rows)
    earlier = jnp.sum(((holder[:, None] == holder[None, :]) & (row[None, :] < row[:, None])).astype(jnp.int32), axis=1)
    return holder * CAP + earlier


def body(inputs, grad_out, lang_ids, lang_block, block_owner, w_in, w_out):
    feat = inputs.shape[1]
    n_lang = lax.axis_size("lang")
    slots = n_lang * CAP
    position = slots_of(lang_ids, lang_block, block_owner)
    onehot = (position[None, :] == jnp.arange(slots)[:, None]).astype(jnp.bfloat16)
    packed = jnp.concatenate([inputs, grad_out], axis=1)
    outgoing = jnp.dot(onehot, packed, preferred_element_type=jnp.float32).astype(jnp.bfloat16)
    outgoing = outgoing.reshape(n_lang, CAP * 2 * feat // 128, 128)
    arrived = lax.all_to_all(outgoing, "lang", split_axis=0, concat_axis=0, tiled=True)
    arrived = arrived.reshape(slots, 2 * feat)
    gathered = lax.all_gather(arrived, "dp", axis=0, tiled=True)
    pre_grad, g_in, g_out = local_grads(gathered[:, :feat], gathered[:, feat:], w_in[0], w_out[0])
    partial_dx = jnp.dot(pre_grad, w_in[0], preferred_element_type=jnp.float32).astype(jnp.bfloat16)
    summed = lax.psum_scatter(partial_dx, "dp", scatter_dimension=0, tiled=True)
    back = summed.reshape(n_lang, CAP * feat // 128, 128)
    returned = lax.all_to_all(back, "lang", split_axis=0, concat_axis=0, tiled=True)
    returned = returned.reshape(slots, feat)
    grad_in = jnp.dot(onehot.T, returned, preferred_element_type=jnp.float32).astype(jnp.bfloat16)
    return (grad_in, g_in[None], g_out[None])


def solution(mesh):
    in_specs = (
        P(("dp", "lang"), None),
        P(("dp", "lang"), None),
        P(("dp", "lang")),
        P(),
        P(),
        P("lang", "dp", None),
        P("lang", "dp", None),
    )
    out_specs = (P(("dp", "lang"), None), P("lang", "dp", None), P("lang", "dp", None))
    return jax.shard_map(body, mesh=mesh, in_specs=in_specs, out_specs=out_specs, check_vma=False)
```

time: 582 us -> 219 us (0.38)
  blocking collectives: 252 us -> 45.8 us
  local copies, waits for them, and re-layouts: 178 us -> 10.2 us
  waiting for transfers between devices: 94.3 us -> 104 us
    all_to_all x1, blocking collectives: 241 us -> 45.8 us  [body(): lax.all_to_all(outgoing, 'lang', split_axis=0, concat_axis=0, tiled=True)]
    scatter x1 -> x0, local copies, waits for them, and re-layouts: 128 us -> none  [body(): outgoing.at[target.reshape(-1)]]
    all_gather x1 -> x0, local copies, waits for them, and re-layouts: 16.4 us -> none  [body(): lax.all_gather(packed[None], 'dp', axis=0, tiled=True)]
    all_gather x1, waiting for transfers between devices: 43.7 us -> 57.2 us  [body(): gathered = lax.all_gather(arrived, 'dp', axis=0, tiled=True)]
    all_to_all x1 -> x0, local copies, waits for them, and re-layouts: 12.9 us -> none  [body(): lax.all_to_all(outgoing.reshape(lang_count, dp_count * per_peer, 2, feat_...]
    all_gather x1 -> x0, blocking collectives: 10.8 us -> none  [body(): lax.all_gather(position[None], 'dp', axis=0, tiled=True)]
    all_to_all x1, waiting for transfers between devices: 12.5 us -> 3.81 us  [body(): lax.all_to_all(back, 'lang', split_axis=0, concat_axis=0, tiled=True)]
    convert_element_type x2 -> x0, local copies, waits for them, and re-layouts: 7.68 us -> none  [the longest x1 5.24 us: body(): partial_dx.astype(jnp.bfloat16)]
  transfers between devices with their start and end apart: 3 -> 3, of which waited for: 3 -> 3; matrix products, arithmetic and copies ran while one was open for 3% -> 6% of each run, Pallas kernels for 0% -> 0%
where the time goes in v1:
time: 219 us; the launch traced here: 218 us
  waiting for transfers between devices  104 us (47%)
  blocking collectives  45.8 us (21%)
  matrix products  31.9 us (15%)
  between operations  14.1 us (6%)
  local copies, waits for them, and re-layouts  10.2 us (5%)
  starting transfers between devices  10.1 us (5%)
    all_gather x1, waiting for transfers between devices, body(): gathered = lax.all_gather(arrived, 'dp', axis=0, tiled=True)  57.2 us
    all_to_all x1, blocking collectives, body(): lax.all_to_all(outgoing, 'lang', split_axis=0, concat_axis=0, tiled=True)  45.8 us
    reduce_scatter x1, waiting for transfers between devices, body(): summed = lax.psum_scatter(partial_dx, 'dp', scatter_dimension=0, tiled=True)  43 us
    all_to_all x1, starting transfers between devices, body(): lax.all_to_all(back, 'lang', split_axis=0, concat_axis=0, tiled=True)  10.1 us
    dot_general x1, matrix products, local_grads(): jnp.dot(pre_grad.T, rows_x, preferred_element_type=jnp.float32)  7.27 us
    dot_general x1, matrix products, local_grads(): jnp.dot(activated.T, rows_g, preferred_element_type=jnp.float32)  6.74 us
    dot_general x1, matrix products, local_grads(): pre_act = jnp.dot(rows_x, w_first.T, preferred_element_type=jnp.float32)  5.03 us
    dot_general x1, matrix products, body(): jnp.dot(pre_grad, w_in[0], preferred_element_type=jnp.float32)  4.66 us
  transfers between devices with their start and end apart: 3, of which 3 were waited for; matrix products, arithmetic and copies ran while one was open for 6% of the time, Pallas kernels for 0%

profile of v1, /device:TPU:32, one launch (start us, length us, event | category | flops | bytes accessed | tf_op | source)
XLA Modules:
  0.0 218.1 jit_solution(15846784867144905162)
XLA Ops:
  7.2 0.0 copy-start
  7.2 0.0 all-gather.2.cloned.1.call-start
  7.2 0.9 select_reduce_fusion.1
  8.2 0.8 select_reduce_fusion
  8.9 0.2 convert_reduce_fusion
  9.1 2.8 %convolution_convert_fusion.1 = bf16[160,4096]{1,0:T(8,128)(2,1)} fusion(bf16[128,2048]{1,0:T(8,128)(2,1)} %param.8, bf16[128,2048]{1,0:T(8,128)(2,1)} %param.7, s32[128]{0:T(128)S(1)} %multiply_add_fusion.1), kind=kOutput, calls=%fused_computation.1 | convolution fusion | flops 170545152 | bytes 2359808 | tf_op jit(solution)/shard_map/dot_general | solution.py:53
  11.9 2.4 %reshape.30 = bf16[32,160,128]{2,1,0:T(8,128)(2,1)S(1)} reshape(bf16[160,4096]{1,0:T(8,128)(2,1)} %convolution_convert_fusion.1) | data formatting | bytes 2621440 | tf_op jit(solution)/shard_map/reshape | solution.py:54
  14.3 45.8 %all_to_all.10 = bf16[32,160,128]{2,1,0:T(8,128)(2,1)} all-to-all(bf16[32,160,128]{2,1,0:T(8,128)(2,1)S(1)} %reshape.30), channel_id=1, replica_groups=mesh['dp'=8,'lang'=32] {'lang'}, dimensions={0} | all-to-all | bytes 2621440 | tf_op jit(solution)/shard_map/all_to_all | solution.py:55
  60.1 3.2 %reshape.31 = bf16[160,4096]{1,0:T(8,128)(2,1)} reshape(bf16[32,160,128]{2,1,0:T(8,128)(2,1)} %all_to_all.10) | data formatting | bytes 2621440 | tf_op jit(solution)/shard_map/reshape | solution.py:56
  63.3 0.0 all-gather.2.cloned.1.call-update
  63.3 0.0 reduce-scatter.2.cloned.1.call-start
  63.4 57.2 %all-gather.2.cloned.1.call-done = bf16[1280,4096]{1,0:T(8,128)(2,1)} async-done(((bf16[160,4096]{1,0:T(8,128)(2,1)}), bf16[1280,4096]{1,0:T(8,128)(2,1)}) %all-gather.2.cloned.1.call-update) | async-done | bytes 10485776 | tf_op jit(solution)/shard_map/all_gather | solution.py:57
  120.6 0.0 copy-done
  120.6 0.0 copy-start.1
  120.6 0.0 copy-start.2
  120.6 5.0 %fusion.2 = f32[1280,512]{1,0:T(8,128)S(1)} fusion(bf16[1280,4096]{1,0:T(8,128)(2,1)} %all-gather.2.cloned.1.call-done, bf16[1,512,2048]{2,1,0:T(8,128)(2,1)S(1)} %copy-done), kind=kOutput, calls=%fused_computation.4 | convolution fusion | flops 2684354560 | bytes 9961472 | tf_op jit(solution)/shard_map/dot_general | solution.py:23
  125.7 0.5 copy-done.1
  126.2 0.6 copy-done.2
  126.8 0.0 copy-start.3
  126.8 4.3 %fusion.11 = bf16[1280,512]{1,0:T(8,128)(2,1)S(1)} fusion(bf16[1280,4096]{1,0:T(8,128)(2,1)S(1)} %copy-done.1, f32[1280,512]{1,0:T(8,128)S(1)} %fusion.2, bf16[1,512,2048]{2,1,0:T(8,128)(2,1)S(1)} %copy-done.2), kind=kOutput, calls=%fused_computation.13 | convolution fusion | flops 2696806400 | bytes 11272192 | tf_op jit(solution)/shard_map/dot_general | solution.py:26
  131.1 0.0 copy-done.3
  131.1 0.0 copy-start.5
  131.1 1.0 copy-done.5
  132.1 4.7 %convolution_convert_fusion = bf16[1280,2048]{1,0:T(8,128)(2,1)} fusion(bf16[1280,512]{1,0:T(8,128)(2,1)S(1)} %fusion.11, bf16[1,512,2048]{2,1,0:T(8,128)(2,1)S(1)} %copy-done), kind=kOutput, calls=%fused_computation | convolution fusion | flops 2686976000 | bytes 8650752 | tf_op jit(solution)/shard_map/dot_general | solution.py:59
  136.8 0.0 reduce-scatter.2.cloned.1.call-update
  136.8 43.0 %reduce-scatter.2.cloned.1.call-done = bf16[160,2048]{1,0:T(8,128)(2,1)} async-done(((bf16[1280,2048]{1,0:T(8,128)(2,1)}), bf16[160,2048]{1,0:T(8,128)(2,1)}) %reduce-scatter.2.cloned.1.call-update) | async-done | bytes 655376 | tf_op jit(solution)/shard_map/reduce_scatter | solution.py:60
  179.8 2.1 reshape.32
  181.9 10.1 %all-to-all-start.1 = ((bf16[32,80,128]{2,1,0:T(8,128)(2,1)}), bf16[32,80,128]{2,1,0:T(8,128)(2,1)S(1)}, u32[]{:S(2)}, u32[]{:S(2)}) async-start(bf16[32,80,128]{2,1,0:T(8,128)(2,1)} %reshape.32), calls=%async_computation.2 | async-start | bytes 1310720 | tf_op jit(solution)/shard_map/all_to_all | solution.py:62
  192.0 0.0 copy-start.4
  192.0 7.3 %fusion.20 = bf16[1,512,2048]{2,1,0:T(8,128)(2,1)} fusion(bf16[1280,512]{1,0:T(8,128)(2,1)} %copy-done.5, bf16[1280,4096]{1,0:T(8,128)(2,1)} %all-gather.2.cloned.1.call-done), kind=kOutput, calls=%fused_computation.16 | convolution fusion | flops 2685403136 | bytes 8650752 | tf_op jit(solution)/shard_map/dot_general | solution.py:29
  199.3 0.0 copy-done.4
  199.3 6.7 %fusion.23 = bf16[1,512,2048]{2,1,0:T(8,128)(2,1)} fusion(bf16[1280,4096]{1,0:T(8,128)(2,1)} %all-gather.2.cloned.1.call-done, f32[1280,512]{1,0:T(8,128)S(1)} %copy-done.4), kind=kOutput, calls=%fused_computation.17 | convolution fusion | flops 2691301376 | bytes 9961472 | tf_op jit(solution)/shard_map/dot_general | solution.py:28
  206.0 3.8 %all-to-all-done.1 = bf16[32,80,128]{2,1,0:T(8,128)(2,1)S(1)} async-done(((bf16[32,80,128]{2,1,0:T(8,128)(2,1)}), bf16[32,80,128]{2,1,0:T(8,128)(2,1)S(1)}, u32[]{:S(2)}, u32[]{:S(2)}) %all-to-all-start.1) | async-done | bytes 655392 | tf_op jit(solution)/shard_map/all_to_all | solution.py:62
  209.8 0.3 reshape.33
  210.1 1.1 convolution_convert_fusion.2
  (1 shorter events, 0.0 us)
Async XLA Ops:
  7.2 113.5 %copy-start = (bf16[1,512,2048]{2,1,0:T(8,128)(2,1)S(1)}, bf16[1,512,2048]{2,1,0:T(8,128)(2,1)}, u32[]{:S(2)}) copy-start(bf16[1,512,2048]{2,1,0:T(8,128)(2,1)} %param.12) | copy-start | bytes 6291460
  7.2 113.4 %all-gather.2.cloned.1.call-start = ((), (), s32[]{:S(2)}) async-start(), calls=%async_computation.3 | async-start | bytes 11796480 | tf_op jit(solution)/shard_map/all_gather | solution.py:57
  63.3 116.5 %reduce-scatter.2.cloned.1.call-start = ((), (), s32[]{:S(2)}) async-start(), calls=%async_computation.4 | async-start | bytes 5898240 | tf_op jit(solution)/shard_map/reduce_scatter | solution.py:60
  120.6 5.5 %copy-start.1 = (bf16[1280,4096]{1,0:T(8,128)(2,1)S(1)}, bf16[1280,4096]{1,0:T(8,128)(2,1)}, u32[]{:S(2)}) copy-start(bf16[1280,4096]{1,0:T(8,128)(2,1)} %all-gather.2.cloned.1.call-done) | copy-start | bytes 31457284
  120.6 6.1 %copy-start.2 = (bf16[1,512,2048]{2,1,0:T(8,128)(2,1)S(1)}, bf16[1,512,2048]{2,1,0:T(8,128)(2,1)}, u32[]{:S(2)}) copy-start(bf16[1,512,2048]{2,1,0:T(8,128)(2,1)} %param.13) | copy-start | bytes 6291460
  126.8 4.3 %copy-start.3 = (f32[1280,512]{1,0:T(8,128)}, f32[1280,512]{1,0:T(8,128)S(1)}, u32[]{:S(2)}) copy-start(f32[1280,512]{1,0:T(8,128)S(1)} %fusion.2) | copy-start | bytes 7864324
  131.1 1.1 copy-start.5
  181.9 27.9 %all-to-all-start.1 = ((bf16[32,80,128]{2,1,0:T(8,128)(2,1)}), bf16[32,80,128]{2,1,0:T(8,128)(2,1)S(1)}, u32[]{:S(2)}, u32[]{:S(2)}) async-start(bf16[32,80,128]{2,1,0:T(8,128)(2,1)} %reshape.32), calls=%async_computation.2 | async-start | bytes 1310720 | tf_op jit(solution)/shard_map/all_to_all | solution.py:62
  192.0 7.3 %copy-start.4 = (f32[1280,512]{1,0:T(8,128)S(1)}, f32[1280,512]{1,0:T(8,128)}, u32[]{:S(2)}) copy-start(f32[1280,512]{1,0:T(8,128)} %copy-done.3) | copy-start | bytes 7864324
Sparse Core Ops, SparseCore 0:
  63.4 57.1 all-gather.1
  136.9 42.8 reduce-scatter.1

commit v2 on v1

v2 whole, which is shorter than its diff:
```python
import functools
import math

import jax
import jax.numpy as jnp
from jax import lax
from jax.experimental import pallas as pl
from jax.experimental.pallas import tpu as pltpu
from jax.sharding import PartitionSpec as P

gelu_scale = math.sqrt(2.0 / math.pi)
CAP = 5
NX, NZ, NY = 4, 8, 4
LANE = 128
SUB = 16
TILES = 16
MESH = pl.DeviceIdType.MESH


def gelu_parts(pre_act):
    tanh_arg = gelu_scale * (pre_act + 0.044715 * pre_act * pre_act * pre_act)
    tangent = jnp.tanh(tanh_arg)
    gelu_value = 0.5 * pre_act * (1.0 + tangent)
    gelu_slope = 0.5 * (1.0 + tangent) + 0.5 * pre_act * (1.0 - tangent * tangent) * gelu_scale * (
        1.0 + 3.0 * 0.044715 * pre_act * pre_act
    )
    return (gelu_value, gelu_slope)


def slots_of(lang_ids, lang_block, block_owner):
    rows = lang_ids.shape[0]
    n_hold = block_owner.shape[0]
    holder_of_lang = jnp.sum(
        jnp.where(lang_block[:, None] == jnp.arange(n_hold)[None, :], block_owner[None, :], 0), axis=1
    )
    holder = jnp.sum(
        jnp.where(lang_ids[:, None] == jnp.arange(lang_block.shape[0])[None, :], holder_of_lang[None, :], 0), axis=1
    )
    row = jnp.arange(rows)
    earlier = jnp.sum(((holder[:, None] == holder[None, :]) & (row[None, :] < row[:, None])).astype(jnp.int32), axis=1)
    return earlier * n_hold + holder


def dot_nt(a, b):
    return lax.dot_general(a, b, (((1,), (1,)), ((), ())), preferred_element_type=jnp.float32)


def dot_nn(a, b):
    return lax.dot_general(a, b, (((1,), (0,)), ((), ())), preferred_element_type=jnp.float32)


def kernel(
    send0, w_in_hbm, w_out_hbm,
    back_ref, gw_in_ref, gw_out_ref,
    w_in, w_out, rx1, rx2, rows, act_t, pg_t, pg, tsend, trecv, own, r1s, r1r, r2s, r2r, fin, bz, bx,
    w_sem, x_send, x_recv, z_send, z_recv, a_send, f_send, h_send, y_recv, c_recv,
    t_send, t_recv, r1_send, r1_recv, r2_send, r2_recv, bz_send, bz_recv, bx_send, bx_recv,
):
    dp, lang = lax.axis_index("dp"), lax.axis_index("lang")
    y, k = dp // 2, dp % 2
    x, z = lang // NZ, lang % NZ
    y_up, y_down, y_far = (y + 1) % NY, (y + NY - 1) % NY, (y + 2) % NY
    up, down, twin = (y_up * 2 + k, lang), (y_down * 2 + k, lang), (y * 2 + 1 - k, lang)
    d_up, d_down, d_far = y_up * 2 + k, y_down * 2 + k, y_far * 2 + k
    x_peers = [(dp, ((x + i) % NX) * NZ + z) for i in range(1, NX)]
    z_peers = [(dp, x * NZ + (z + i) % NZ) for i in range(1, NZ)]

    def send(src, dst, s_sem, r_sem, to):
        pltpu.make_async_remote_copy(
            src_ref=src, dst_ref=dst, send_sem=s_sem, recv_sem=r_sem, device_id=to, device_id_type=MESH
        ).start()

    def take(ref, sem):
        pltpu.make_async_copy(ref, ref, sem).wait()

    w_copies = [
        pltpu.make_async_copy(w_in_hbm, w_in, w_sem.at[0]),
        pltpu.make_async_copy(w_out_hbm, w_out, w_sem.at[1]),
    ]
    for copy in w_copies:
        copy.start()

    barrier = pltpu.get_barrier_semaphore()
    peers = [up, down, twin, *x_peers, *z_peers]
    for peer in peers:
        pl.semaphore_signal(barrier, inc=1, device_id=peer, device_id_type=MESH)
    pl.semaphore_wait(barrier, len(peers))

    big_row = lax.broadcasted_iota(jnp.int32, (SUB * TILES, SUB * TILES), 0)
    big_col = lax.broadcasted_iota(jnp.int32, (SUB * TILES, SUB * TILES), 1)
    swap = jnp.where(big_col == (big_row % SUB) * TILES + big_row // SUB, 1.0, 0.0).astype(jnp.bfloat16)

    def start_x(c):
        pltpu.make_async_copy(send0.at[c, x], rx1.at[c, x], x_recv.at[c]).start()
        for i in range(1, NX):
            to = (x + i) % NX
            send(send0.at[c, to], rx1.at[c, x], x_send.at[c], x_recv.at[c], (dp, to * NZ + z))

    def start_z(c):
        take(rx1.at[c], x_recv.at[c])
        pltpu.make_async_copy(rx1.at[c, :, z], rx2.at[c, z], z_recv.at[c]).start()
        for i in (4, 3, 5, 2, 6, 1, 7):
            to = (z + i) % NZ
            send(rx1.at[c, :, to], rx2.at[c, z], z_send.at[c], z_recv.at[c], (dp, x * NZ + to))

    def start_gather(c):
        take(rx2.at[c], z_recv.at[c])
        for g in range(2):
            tiles = rx2[c, 4 * g : 4 * g + 4].reshape(SUB, 2 * TILES, LANE)
            tx = tiles[:, :TILES].reshape(SUB * TILES, LANE)
            tg = tiles[:, TILES:].reshape(SUB * TILES, LANE)
            both = dot_nn(swap, jnp.concatenate([tx, tg], axis=1)).astype(jnp.bfloat16)
            for j in range(TILES):
                part = both[j * SUB : (j + 1) * SUB]
                rows[c, dp, g * SUB : (g + 1) * SUB, j * LANE : (j + 1) * LANE] = part[:, :LANE]
                rows[c, dp, g * SUB : (g + 1) * SUB, (TILES + j) * LANE : (TILES + j + 1) * LANE] = part[:, LANE:]
        mine = rows.at[c, dp]
        send(mine, mine, a_send.at[c], y_recv.at[c, 0], up)
        send(mine, mine, a_send.at[c], y_recv.at[c, 1], down)
        send(mine, mine, a_send.at[c], c_recv.at[c, 0], twin)

    def forward(c):
        low, high = pl.ds(0, SUB), pl.ds(SUB, SUB)
        take(rows.at[c, d_down], y_recv.at[c, 0])
        block = rows.at[c, d_down, low]
        send(block, block, f_send.at[c], y_recv.at[c, 2], up)
        take(rows.at[c, d_up], y_recv.at[c, 1])
        block = rows.at[c, d_up, high]
        send(block, block, f_send.at[c], y_recv.at[c, 3], down)
        send(rows.at[c, d_down], rows.at[c, d_down], f_send.at[c], c_recv.at[c, 1], twin)
        send(rows.at[c, d_up], rows.at[c, d_up], f_send.at[c], c_recv.at[c, 2], twin)

    def forward_far(c):
        for i in range(2):
            block = rows.at[c, d_far, pl.ds(i * SUB, SUB)]
            take(block, y_recv.at[c, 2 + i])
            send(block, block, h_send.at[c], c_recv.at[c, 3], twin)

    def compute(c):
        t_own, t_down = y * 2 + 1 - k, y_down * 2 + 1 - k
        t_up, t_far = y_up * 2 + 1 - k, y_far * 2 + 1 - k
        for i, d in enumerate((t_own, t_down, t_up, t_far)):
            take(rows.at[c, d], c_recv.at[c, i])
        hid, feat = w_in.shape

        def hidden(f, _):
            at = pl.ds(pl.multiple_of(f * 256, 256), 256)
            x_rows = rows[c, :, :, :feat].reshape(2 * NY * 32, feat)
            g_rows = rows[c, :, :, feat:].reshape(2 * NY * 32, feat)
            value, slope = gelu_parts(dot_nt(x_rows, w_in[at, :]))
            pre_grad = (dot_nt(g_rows, w_out[at, :]) * slope).astype(jnp.bfloat16)
            act_t[c, at] = value.astype(jnp.bfloat16).T
            pg_t[c, at] = pre_grad.T
            pg[:, :, :, at] = pre_grad.reshape(NY, 2, 32, 256)
            return 0

        lax.fori_loop(0, hid // 256, hidden, 0)

        def away(f, _):
            at = pl.ds(pl.multiple_of(f * 512, 512), 512)
            part = dot_nn(pg[:, 1 - k].reshape(NY * 32, hid), w_in[:, at])
            tsend[c, :, :, at] = part.astype(jnp.bfloat16).reshape(NY, 32, 512)
            return 0

        lax.fori_loop(0, feat // 512, away, 0)
        send(tsend.at[c], trecv.at[c], t_send.at[c], t_recv.at[c], twin)

        def home(f, _):
            at = pl.ds(pl.multiple_of(f * 512, 512), 512)
            own[c % 4, :, :, at] = dot_nn(pg[:, k].reshape(NY * 32, hid), w_in[:, at]).reshape(NY, 32, 512)
            return 0

        lax.fori_loop(0, feat // 512, home, 0)

    def reduce_far(c):
        take(trecv.at[c], t_recv.at[c])
        o = c % 4
        for i in range(2):
            at = pl.ds(i * SUB, SUB)
            r1s[c, i] = (own[o, y_far, at] + trecv[c, y_far, at].astype(jnp.float32)).astype(jnp.bfloat16)
        send(r1s.at[c, 0], r1r.at[c, 0], r1_send.at[c], r1_recv.at[c, 0], up)
        send(r1s.at[c, 1], r1r.at[c, 1], r1_send.at[c], r1_recv.at[c, 1], down)

    def reduce_near(c):
        o = c % 4
        for i, (to, y_to, first) in enumerate(((up, y_up, 0), (down, y_down, SUB))):
            take(r1r.at[c, i], r1_recv.at[c, i])
            with_far, alone = pl.ds(first, SUB), pl.ds(SUB - first, SUB)
            total = own[o, y_to, with_far] + trecv[c, y_to, with_far].astype(jnp.float32)
            r2s[c, i, with_far] = (total + r1r[c, i].astype(jnp.float32)).astype(jnp.bfloat16)
            total = own[o, y_to, alone] + trecv[c, y_to, alone].astype(jnp.float32)
            r2s[c, i, alone] = total.astype(jnp.bfloat16)
            send(r2s.at[c, i], r2r.at[c, i], r2_send.at[c], r2_recv.at[c, i], to)
        own_sum = own[o, y] + trecv[c, y].astype(jnp.float32)
        own[o, y] = own_sum

    def reduce_last(c):
        o = c % 4
        for i in range(2):
            take(r2r.at[c, i], r2_recv.at[c, i])
        for g in range(2):
            at = pl.ds(g * SUB, SUB)
            total = own[o, y, at] + r2r[c, 0, at].astype(jnp.float32) + r2r[c, 1, at].astype(jnp.float32)
            total = total.astype(jnp.bfloat16)
            tall = jnp.concatenate([total[:, j * LANE : (j + 1) * LANE] for j in range(TILES)], axis=0)
            out = dot_nn(swap, tall).astype(jnp.bfloat16)
            fin[c, 4 * g : 4 * g + 4] = out.reshape(4, NX, TILES, LANE)
        pltpu.make_async_copy(fin.at[c, z], bz.at[c, z], bz_recv.at[c]).start()
        for i in (4, 3, 5, 2, 6, 1, 7):
            to = (z + i) % NZ
            send(fin.at[c, to], bz.at[c, z], bz_send.at[c], bz_recv.at[c], (dp, x * NZ + to))

    def start_back_x(c):
        take(bz.at[c], bz_recv.at[c])
        pltpu.make_async_copy(bz.at[c, :, x], bx.at[c, x], bx_recv.at[c]).start()
        for i in range(1, NX):
            to = (x + i) % NX
            send(bz.at[c, :, to], bx.at[c, x], bx_send.at[c], bx_recv.at[c], (dp, to * NZ + z))

    def finish(c):
        take(bx.at[c], bx_recv.at[c])
        for g in range(2):
            tall = bx[c, 2 * g : 2 * g + 2].reshape(SUB * TILES, LANE)
            out = dot_nn(swap, tall).astype(jnp.bfloat16)
            for j in range(TILES):
                back_ref[c, g * SUB : (g + 1) * SUB, j * LANE : (j + 1) * LANE] = out[j * SUB : (j + 1) * SUB]

    def weight_grads(f):
        feat = w_in.shape[1]
        at = pl.ds(pl.multiple_of(f * 256, 256), 256)
        at_g = pl.ds(pl.multiple_of(feat + f * 256, 256), 256)
        total_in = total_out = None
        for c in range(CAP):
            part_in = dot_nn(pg_t[c], rows[c, :, :, at].reshape(2 * NY * 32, 256))
            part_out = dot_nn(act_t[c], rows[c, :, :, at_g].reshape(2 * NY * 32, 256))
            total_in = part_in if c == 0 else total_in + part_in
            total_out = part_out if c == 0 else total_out + part_out
        gw_in_ref[:, at] = total_in.astype(jnp.bfloat16)
        gw_out_ref[:, at] = total_out.astype(jnp.bfloat16)

    start_x(0)
    start_x(1)

    stages = [
        (0, start_z),
        (1, start_gather),
        (2, forward),
        (4, reduce_far),
        (5, reduce_near),
        (6, reduce_last),
        (7, start_back_x),
        (8, finish),
        (2, forward_far),
        (3, compute),
    ]

    def tick(t, _):
        for offset, stage in stages[:1]:
            pl.when((t >= offset) & (t < offset + CAP))(functools.partial(stage, t - offset))
        pl.when(t + 2 < CAP)(lambda: start_x(t + 2))
        for offset, stage in stages[1:]:
            if stage is compute:
                @pl.when(t == 3)
                def _():
                    for copy in w_copies:
                        copy.wait()
            pl.when((t >= offset) & (t < offset + CAP))(functools.partial(stage, t - offset))

        @pl.when((t >= 8) & (t < 12))
        def _():
            lax.fori_loop(0, 2, lambda i, _: (weight_grads((t - 8) * 2 + i), 0)[1], 0)

        return 0

    lax.fori_loop(0, 8 + CAP, tick, 0)

    def drain(c, _):
        take(rx1.at[c, pl.ds(0, NX - 1)], x_send.at[c])
        take(rx2.at[c, pl.ds(0, NZ - 1)], z_send.at[c])
        take(rows.at[c, pl.ds(0, 3)], a_send.at[c])
        take(rows.at[c, pl.ds(0, 3)], f_send.at[c])
        take(rows.at[c, 0], h_send.at[c])
        take(tsend.at[c], t_send.at[c])
        take(r1s.at[c], r1_send.at[c])
        take(r2s.at[c], r2_send.at[c])
        take(fin.at[c, pl.ds(0, NZ - 1)], bz_send.at[c])
        take(bx.at[c, pl.ds(0, NX - 1)], bx_send.at[c])
        return 0

    lax.fori_loop(0, CAP, drain, 0)


def exchange_and_compute(outgoing, w_first, w_second):
    hid, feat = w_first.shape
    bf16, f32 = jnp.bfloat16, jnp.float32
    vmem = pl.BlockSpec(memory_space=pltpu.VMEM)
    dma = pltpu.SemaphoreType.DMA
    return pl.pallas_call(
        kernel,
        out_shape=(
            jax.ShapeDtypeStruct((CAP, NX * NZ, feat), bf16),
            jax.ShapeDtypeStruct((hid, feat), bf16),
            jax.ShapeDtypeStruct((hid, feat), bf16),
        ),
        in_specs=[vmem, pl.BlockSpec(memory_space=pl.ANY), pl.BlockSpec(memory_space=pl.ANY)],
        out_specs=(vmem, vmem, vmem),
        scratch_shapes=[
            pltpu.VMEM((hid, feat), bf16),
            pltpu.VMEM((hid, feat), bf16),
            pltpu.VMEM((CAP, NX, NZ, 2 * TILES, LANE), bf16),
            pltpu.VMEM((CAP, NZ, NX, 2 * TILES, LANE), bf16),
            pltpu.VMEM((CAP, 2 * NY, 32, 2 * feat), bf16),
            pltpu.VMEM((CAP, hid, 256), bf16),
            pltpu.VMEM((CAP, hid, 256), bf16),
            pltpu.VMEM((NY, 2, 32, hid), bf16),
            pltpu.VMEM((CAP, NY, 32, feat), bf16),
            pltpu.VMEM((CAP, NY, 32, feat), bf16),
            pltpu.VMEM((4, NY, 32, feat), f32),
            pltpu.VMEM((CAP, 2, SUB, feat), bf16),
            pltpu.VMEM((CAP, 2, SUB, feat), bf16),
            pltpu.VMEM((CAP, 2, 32, feat), bf16),
            pltpu.VMEM((CAP, 2, 32, feat), bf16),
            pltpu.VMEM((CAP, NZ, NX, TILES, LANE), bf16),
            pltpu.VMEM((CAP, NZ, NX, TILES, LANE), bf16),
            pltpu.VMEM((CAP, NX, NZ, TILES, LANE), bf16),
            dma((2,)),
            dma((CAP,)), dma((CAP,)), dma((CAP,)), dma((CAP,)),
            dma((CAP,)), dma((CAP,)), dma((CAP,)),
            dma((CAP, 4)), dma((CAP, 4)),
            dma((CAP,)), dma((CAP,)),
            dma((CAP,)), dma((CAP, 2)),
            dma((CAP,)), dma((CAP, 2)),
            dma((CAP,)), dma((CAP,)), dma((CAP,)), dma((CAP,)),
        ],
        compiler_params=pltpu.CompilerParams(
            collective_id=0, has_side_effects=True, vmem_limit_bytes=50 * 1024 * 1024
        ),
    )(outgoing, w_first, w_second)


def body(inputs, grad_out, lang_ids, lang_block, block_owner, w_in, w_out):
    feat = inputs.shape[1]
    slots = CAP * NX * NZ
    position = slots_of(lang_ids, lang_block, block_owner)
    onehot = (position[None, :] == jnp.arange(slots)[:, None]).astype(jnp.bfloat16)
    packed = jnp.concatenate([inputs, grad_out], axis=1)
    outgoing = jnp.dot(onehot, packed, preferred_element_type=jnp.float32).astype(jnp.bfloat16)
    outgoing = outgoing.reshape(CAP, NX, NZ, 2 * TILES, LANE)
    back, g_in, g_out = exchange_and_compute(outgoing, w_in[0], w_out[0])
    grad_in = jnp.dot(onehot.T, back.reshape(slots, feat), preferred_element_type=jnp.float32).astype(jnp.bfloat16)
    return (grad_in, g_in[None], g_out[None])


def solution(mesh):
    in_specs = (
        P(("dp", "lang"), None),
        P(("dp", "lang"), None),
        P(("dp", "lang")),
        P(),
        P(),
        P("lang", "dp", None),
        P("lang", "dp", None),
    )
    out_specs = (P(("dp", "lang"), None), P("lang", "dp", None), P("lang", "dp", None))
    return jax.shard_map(body, mesh=mesh, in_specs=in_specs, out_specs=out_specs, check_vma=False)
```

time: 219 us -> 125 us (0.57)
  Pallas kernels: 0 us -> 115 us
  waiting for transfers between devices: 104 us -> 0 us
  blocking collectives: 45.8 us -> 0 us
  matrix products: 31.9 us -> 2.84 us
  between operations: 14.1 us -> 0.67 us
  starting transfers between devices: 10.1 us -> 0 us
  local copies, waits for them, and re-layouts: 10.2 us -> 3.94 us
    pallas_call x0 -> x1, Pallas kernels: none -> 115 us  [exchange_and_compute(): pl.pallas_call(kernel, out_shape=(jax.ShapeDtypeStruct((CAP, NX * NZ, fea...]
    all_gather x1 -> x0, waiting for transfers between devices: 57.2 us -> none  [body(): gathered = lax.all_gather(arrived, 'dp', axis=0, tiled=True)]
    all_to_all x1 -> x0, blocking collectives: 45.8 us -> none  [body(): lax.all_to_all(outgoing, 'lang', split_axis=0, concat_axis=0, tiled=True)]
    reduce_scatter x1 -> x0, waiting for transfers between devices: 43 us -> none  [body(): summed = lax.psum_scatter(partial_dx, 'dp', scatter_dimension=0, tiled=True)]
    dot_general x6 -> x1, matrix products: 29.1 us -> 1.14 us  [body(): jnp.dot(onehot.T, back.reshape(slots, feat), preferred_element_type=jnp.f...]
    all_to_all x1 -> x0, starting transfers between devices: 10.1 us -> none  [body(): lax.all_to_all(back, 'lang', split_axis=0, concat_axis=0, tiled=True)]
    reshape x4 -> x0, local copies, waits for them, and re-layouts: 8.04 us -> none  [the longest x1 3.24 us: body(): arrived = arrived.reshape(slots, 2 * feat)]
    all_to_all x1 -> x0, waiting for transfers between devices: 3.81 us -> none  [body(): lax.all_to_all(back, 'lang', split_axis=0, concat_axis=0, tiled=True)]
  transfers between devices with their start and end apart: 3 -> 0, of which waited for: 3 -> 0; matrix products, arithmetic and copies ran while one was open for 6% -> 0% of each run, Pallas kernels for 0% -> 0%
where the time goes in v2:
time: 125 us; the launch traced here: 124 us
  Pallas kernels  115 us (92%)
  local copies, waits for them, and re-layouts  3.94 us (3%)
  matrix products  2.84 us (2%)
  other arithmetic  1.73 us (1%)
    pallas_call x1, Pallas kernels, exchange_and_compute(): pl.pallas_call(kernel, out_shape=(jax.ShapeDtypeStruct((CAP, NX * NZ, fea...  115 us
    unnamed x5, local copies, waits for them, and re-layouts  3.94 us

profile of v2, /device:TPU:32, one launch (start us, length us, event | category | flops | bytes accessed | tf_op | source)
XLA Modules:
  0.0 123.9 jit_solution(17537665765104157655)
XLA Ops:
  0.6 0.8 select_reduce_fusion.1
  1.4 0.8 select_reduce_fusion
  2.2 0.2 convert_reduce_fusion
  2.4 1.7 %fusion = bf16[20,8,32,128]{3,1,2,0:T(8,128)(2,1)S(1)} fusion(bf16[128,2048]{1,0:T(8,128)(2,1)} %param.8, bf16[128,2048]{1,0:T(8,128)(2,1)} %param.7, s32[128]{0:T(128)S(1)} %multiply_add_fusion), kind=kOutput, calls=%fused_computation.2 | convolution fusion | flops 170545152 | bytes 2359808 | tf_op jit(solution)/shard_map/dot_general | solution.py:347
  4.1 0.3 copy.10
  4.4 114.8 %shard_map.94 = (bf16[5,32,2048]{2,1,0:T(8,128)(2,1)S(1)}, bf16[512,2048]{1,0:T(8,128)(2,1)S(1)}, bf16[512,2048]{1,0:T(8,128)(2,1)}) custom-call(bf16[5,4,8,32,128]{4,3,2,1,0:T(8,128)(2,1)S(1)} %bitcast.10, bf16[512,2048]{1,0:T(8,128)(2,1)} %bitcast.13, bf16[512,2048]{1,0:T(8,128)(2,1)} %bitcast.14), custom_call_target="tpu_custom_call" | custom-call | tf_op jit(solution)/shard_map/pallas_call | solution.py:298
  119.1 1.1 convolution_convert_fusion.1
  120.3 0.0 copy-start
  120.3 1.3 %copy.13 = bf16[1,512,2048]{2,1,0:T(8,128)(2,1)} copy(bf16[1,512,2048]{2,1,0:T(8,128)(2,1)S(1)} %bitcast.11) | data formatting | bytes 4194304
  121.6 1.0 copy-done
  122.6 1.3 %copy.14 = bf16[1,512,2048]{2,1,0:T(8,128)(2,1)} copy(bf16[1,512,2048]{2,1,0:T(8,128)(2,1)S(1)} %bitcast.15) | data formatting | bytes 4194304
  (1 shorter events, 0.0 us)
Async XLA Ops:
  120.3 2.3 %copy-start = (bf16[512,2048]{1,0:T(8,128)(2,1)S(1)}, bf16[512,2048]{1,0:T(8,128)(2,1)}, u32[]{:S(2)}) copy-start(bf16[512,2048]{1,0:T(8,128)(2,1)} %get-tuple-element.8) | copy-start | bytes 6291460

commit v3 on v2

v3 whole, which is shorter than its diff:
```python
import functools
import math

import jax
import jax.numpy as jnp
from jax import lax
from jax.experimental import pallas as pl
from jax.experimental.pallas import tpu as pltpu
from jax.sharding import PartitionSpec as P

gelu_scale = math.sqrt(2.0 / math.pi)
CAP = 5
NX, NZ, NY = 4, 8, 4
LANE = 128
SUB = 16
TILES = 16
MESH = pl.DeviceIdType.MESH


def gelu_parts(pre_act):
    tanh_arg = gelu_scale * (pre_act + 0.044715 * pre_act * pre_act * pre_act)
    tangent = jnp.tanh(tanh_arg)
    gelu_value = 0.5 * pre_act * (1.0 + tangent)
    gelu_slope = 0.5 * (1.0 + tangent) + 0.5 * pre_act * (1.0 - tangent * tangent) * gelu_scale * (
        1.0 + 3.0 * 0.044715 * pre_act * pre_act
    )
    return (gelu_value, gelu_slope)


def placement(route, swap_type):
    n_hold = NX * NZ

    def picks(shape, values):
        at = lax.broadcasted_iota(jnp.int32, shape, 0)
        return jnp.where(at == values, 1.0, 0.0).astype(swap_type)

    lang_of_row = picks((256, 128), route[:, 384:512])
    block_of_lang = dot_nn(picks((128, 256), route[:, 0:256]), lang_of_row).astype(swap_type)
    holder = dot_nn(picks((n_hold, 128), route[:, 256:384]), block_of_lang)
    row = lax.broadcasted_iota(jnp.int32, (128, 128), 0)
    later = lax.broadcasted_iota(jnp.int32, (128, 128), 1)
    before = jnp.where(row < later, 1.0, 0.0).astype(swap_type)
    earlier = dot_nn(holder.astype(swap_type), before)
    return [jnp.where(earlier == float(slot), holder, 0.0).astype(swap_type) for slot in range(CAP)]


def dot_nt(a, b):
    return lax.dot_general(a, b, (((1,), (1,)), ((), ())), preferred_element_type=jnp.float32)


def dot_nn(a, b):
    return lax.dot_general(a, b, (((1,), (0,)), ((), ())), preferred_element_type=jnp.float32)


def kernel(
    route_ref, x_hbm, g_hbm, w_in_hbm, w_out_hbm,
    grad_ref, gw_in_ref, gw_out_ref,
    x_ref, g_ref, w_in, w_out, place, total_ref, out_tiles, in_tiles, rows, act_t, pg_t, pg, slots, tsend, trecv, own, r1s, r1r, r2s, r2r, fin, back,
    w_sem, e_send, e_recv, a_send, f_send, h_send, y_recv, c_recv,
    t_send, t_recv, r1_send, r1_recv, r2_send, r2_recv, b_send, b_recv,
):
    dp, lang = lax.axis_index("dp"), lax.axis_index("lang")
    y, k = dp // 2, dp % 2
    n_hold = NX * NZ
    y_up, y_down, y_far = (y + 1) % NY, (y + NY - 1) % NY, (y + 2) % NY
    up, down, twin = (y_up * 2 + k, lang), (y_down * 2 + k, lang), (y * 2 + 1 - k, lang)
    d_up, d_down, d_far = y_up * 2 + k, y_down * 2 + k, y_far * 2 + k
    def send(src, dst, s_sem, r_sem, to):
        pltpu.make_async_remote_copy(
            src_ref=src, dst_ref=dst, send_sem=s_sem, recv_sem=r_sem, device_id=to, device_id_type=MESH
        ).start()

    def take(ref, sem):
        pltpu.make_async_copy(ref, ref, sem).wait()

    w_copies = [
        pltpu.make_async_copy(w_in_hbm, w_in, w_sem.at[0]),
        pltpu.make_async_copy(w_out_hbm, w_out, w_sem.at[1]),
    ]
    row_copies = [
        pltpu.make_async_copy(x_hbm, x_ref, w_sem.at[2]),
        pltpu.make_async_copy(g_hbm, g_ref, w_sem.at[3]),
    ]
    for copy in (*row_copies, *w_copies):
        copy.start()

    barrier = pltpu.get_barrier_semaphore()
    for peer in (up, down, twin):
        pl.semaphore_signal(barrier, inc=1, device_id=peer, device_id_type=MESH)

    def greet(i, _):
        pl.semaphore_signal(barrier, inc=1, device_id=(dp, (lang + i) % n_hold), device_id_type=MESH)
        return 0

    lax.fori_loop(1, n_hold, greet, 0)
    big_row = lax.broadcasted_iota(jnp.int32, (SUB * TILES, SUB * TILES), 0)
    big_col = lax.broadcasted_iota(jnp.int32, (SUB * TILES, SUB * TILES), 1)
    swap = jnp.where(big_col == (big_row % SUB) * TILES + big_row // SUB, 1.0, 0.0).astype(jnp.bfloat16)

    feat = w_in.shape[1]
    hid = w_in.shape[0]
    for slot, picked in enumerate(placement(route_ref[...], jnp.bfloat16)):
        place[slot] = picked

    def to_tiles(matrix, width):
        return jnp.concatenate([matrix[:, j * LANE : (j + 1) * LANE] for j in range(width)], axis=0)

    def dispatch(c):
        x_rows = dot_nn(place[c], x_ref[...]).astype(jnp.bfloat16)
        g_rows = dot_nn(place[c], g_ref[...]).astype(jnp.bfloat16)
        for g in range(2):
            at = slice(g * SUB, (g + 1) * SUB)
            both = jnp.concatenate([to_tiles(x_rows[at], TILES), to_tiles(g_rows[at], TILES)], axis=1)
            both = dot_nn(swap, both).astype(jnp.bfloat16)
            out_tiles[c, at, :TILES] = both[:, :LANE].reshape(SUB, TILES, LANE)
            out_tiles[c, at, TILES:] = both[:, LANE:].reshape(SUB, TILES, LANE)

    def start_exchange(c):
        pltpu.make_async_copy(out_tiles.at[c, lang], in_tiles.at[c, lang], e_recv.at[c]).start()

        def one(i, _):
            to = (lang + i) % n_hold
            send(out_tiles.at[c, to], in_tiles.at[c, lang], e_send.at[c], e_recv.at[c], (dp, to))
            return 0

        lax.fori_loop(1, n_hold, one, 0)

    def start_next(c):
        @pl.when(c + 1 < CAP)
        def _():
            start_exchange(c + 1)

    def prepare(c):
        @pl.when(c + 2 < CAP)
        def _():
            dispatch(c + 2)

    def start_gather(c):
        take(in_tiles.at[c], e_recv.at[c])
        start_next(c)
        for g in range(2):
            tiles = in_tiles[c, g * SUB : (g + 1) * SUB]
            tx = tiles[:, :TILES].reshape(SUB * TILES, LANE)
            tg = tiles[:, TILES:].reshape(SUB * TILES, LANE)
            both = dot_nn(swap, jnp.concatenate([tx, tg], axis=1)).astype(jnp.bfloat16)
            for j in range(TILES):
                part = both[j * SUB : (j + 1) * SUB]
                rows[c, dp, g * SUB : (g + 1) * SUB, j * LANE : (j + 1) * LANE] = part[:, :LANE]
                rows[c, dp, g * SUB : (g + 1) * SUB, (TILES + j) * LANE : (TILES + j + 1) * LANE] = part[:, LANE:]
        mine = rows.at[c, dp]
        send(mine, mine, a_send.at[c], y_recv.at[c, 0], up)
        send(mine, mine, a_send.at[c], y_recv.at[c, 1], down)
        send(mine, mine, a_send.at[c], c_recv.at[c, 0], twin)

    def forward(c):
        low, high = pl.ds(0, SUB), pl.ds(SUB, SUB)
        take(rows.at[c, d_down], y_recv.at[c, 0])
        block = rows.at[c, d_down, low]
        send(block, block, f_send.at[c], y_recv.at[c, 2], up)
        take(rows.at[c, d_up], y_recv.at[c, 1])
        block = rows.at[c, d_up, high]
        send(block, block, f_send.at[c], y_recv.at[c, 3], down)
        send(rows.at[c, d_down], rows.at[c, d_down], f_send.at[c], c_recv.at[c, 1], twin)
        send(rows.at[c, d_up], rows.at[c, d_up], f_send.at[c], c_recv.at[c, 2], twin)

    def forward_far(c):
        for i in range(2):
            block = rows.at[c, d_far, pl.ds(i * SUB, SUB)]
            take(block, y_recv.at[c, 2 + i])
            send(block, block, h_send.at[c], c_recv.at[c, 3], twin)

    def compute(c):
        t_own, t_down = y * 2 + 1 - k, y_down * 2 + 1 - k
        t_up, t_far = y_up * 2 + 1 - k, y_far * 2 + 1 - k
        for i, d in enumerate((t_own, t_down, t_up, t_far)):
            take(rows.at[c, d], c_recv.at[c, i])

        def hidden(f, _):
            at = pl.ds(pl.multiple_of(f * 256, 256), 256)
            x_rows = rows[c, :, :, :feat].reshape(2 * NY * 32, feat)
            g_rows = rows[c, :, :, feat:].reshape(2 * NY * 32, feat)
            value, slope = gelu_parts(dot_nt(x_rows, w_in[at, :]))
            pre_grad = (dot_nt(g_rows, w_out[at, :]) * slope).astype(jnp.bfloat16)
            act_t[c, at] = value.astype(jnp.bfloat16).T
            pg_t[c, at] = pre_grad.T
            pre_grad = pre_grad.reshape(NY, 2, 32, 256)
            for core in range(2):
                pg[(core + k) % 2, :, :, at] = pre_grad[:, core]
            return 0

        lax.fori_loop(0, hid // 256, hidden, 0)

        def rows_grad(f, _):
            at = pl.ds(pl.multiple_of(f * 512, 512), 512)
            part = dot_nn(pg[...].reshape(2 * NY * 32, hid), w_in[:, at]).reshape(2, NY, 32, 512)
            own[c % 4, :, :, at] = part[0]
            tsend[c, :, :, at] = part[1].astype(jnp.bfloat16)
            return 0

        lax.fori_loop(0, feat // 512, rows_grad, 0)
        send(tsend.at[c], trecv.at[c], t_send.at[c], t_recv.at[c], twin)

    def reduce_far(c):
        take(trecv.at[c], t_recv.at[c])
        o = c % 4
        for i in range(2):
            at = pl.ds(i * SUB, SUB)
            r1s[c, i] = (own[o, y_far, at] + trecv[c, y_far, at].astype(jnp.float32)).astype(jnp.bfloat16)
        send(r1s.at[c, 0], r1r.at[c, 0], r1_send.at[c], r1_recv.at[c, 0], up)
        send(r1s.at[c, 1], r1r.at[c, 1], r1_send.at[c], r1_recv.at[c, 1], down)

    def reduce_near(c):
        o = c % 4
        for i, (to, y_to, first) in enumerate(((up, y_up, 0), (down, y_down, SUB))):
            take(r1r.at[c, i], r1_recv.at[c, i])
            with_far, alone = pl.ds(first, SUB), pl.ds(SUB - first, SUB)
            total = own[o, y_to, with_far] + trecv[c, y_to, with_far].astype(jnp.float32)
            r2s[c, i, with_far] = (total + r1r[c, i].astype(jnp.float32)).astype(jnp.bfloat16)
            total = own[o, y_to, alone] + trecv[c, y_to, alone].astype(jnp.float32)
            r2s[c, i, alone] = total.astype(jnp.bfloat16)
            send(r2s.at[c, i], r2r.at[c, i], r2_send.at[c], r2_recv.at[c, i], to)
        own_sum = own[o, y] + trecv[c, y].astype(jnp.float32)
        own[o, y] = own_sum

    def reduce_last(c):
        o = c % 4
        for i in range(2):
            take(r2r.at[c, i], r2_recv.at[c, i])
        for g in range(2):
            at = pl.ds(g * SUB, SUB)
            total = own[o, y, at] + r2r[c, 0, at].astype(jnp.float32) + r2r[c, 1, at].astype(jnp.float32)
            total = total.astype(jnp.bfloat16)
            out = dot_nn(swap, to_tiles(total, TILES)).astype(jnp.bfloat16)
            fin[c, g * SUB : (g + 1) * SUB] = out.reshape(SUB, TILES, LANE)
        pltpu.make_async_copy(fin.at[c, lang], back.at[c, lang], b_recv.at[c]).start()

        def one(i, _):
            to = (lang + i) % n_hold
            send(fin.at[c, to], back.at[c, lang], b_send.at[c], b_recv.at[c], (dp, to))
            return 0

        lax.fori_loop(1, n_hold, one, 0)

    def finish(c):
        take(back.at[c], b_recv.at[c])
        tall = jnp.concatenate([back[c, g * SUB : (g + 1) * SUB].reshape(SUB * TILES, LANE) for g in range(2)], axis=1)
        flat = dot_nn(swap, tall).astype(jnp.bfloat16)
        for g in range(2):
            for j in range(TILES):
                at = slice(g * LANE, (g + 1) * LANE)
                slots[g * SUB : (g + 1) * SUB, j * LANE : (j + 1) * LANE] = flat[j * SUB : (j + 1) * SUB, at]

        def add(f, _):
            at = pl.ds(pl.multiple_of(f * 512, 512), 512)
            part = lax.dot_general(
                place[c], slots[:, at], (((0,), (0,)), ((), ())), preferred_element_type=jnp.float32
            )
            grad_ref[:, at] = (total_ref[:, at] + part).astype(jnp.bfloat16)
            total_ref[:, at] = total_ref[:, at] + part
            return 0

        lax.fori_loop(0, feat // 512, add, 0)

    def weight_grads(f):
        at = pl.ds(pl.multiple_of(f * 256, 256), 256)
        at_g = pl.ds(pl.multiple_of(feat + f * 256, 256), 256)
        total_in = total_out = None
        for c in range(CAP):
            part_in = dot_nn(pg_t[c], rows[c, :, :, at].reshape(2 * NY * 32, 256))
            part_out = dot_nn(act_t[c], rows[c, :, :, at_g].reshape(2 * NY * 32, 256))
            total_in = part_in if c == 0 else total_in + part_in
            total_out = part_out if c == 0 else total_out + part_out
        gw_in_ref[:, at] = total_in.astype(jnp.bfloat16)
        gw_out_ref[:, at] = total_out.astype(jnp.bfloat16)

    for copy in row_copies:
        copy.wait()
    dispatch(0)
    pl.semaphore_wait(barrier, n_hold - 1 + 3)
    start_exchange(0)
    dispatch(1)
    total_ref[...] = jnp.zeros_like(total_ref)

    stages = [
        (0, start_gather),
        (1, forward),
        (0, prepare),
        (2, compute),
        (1, forward_far),
        (3, reduce_far),
        (4, reduce_near),
        (5, reduce_last),
        (6, finish),
    ]

    def tick(t, _):
        @pl.when(t == 2)
        def _():
            for copy in w_copies:
                copy.wait()

        for offset, stage in stages:
            pl.when((t >= offset) & (t < offset + CAP))(functools.partial(stage, t - offset))

        @pl.when((t >= 7) & (t < 11))
        def _():
            lax.fori_loop(0, 2, lambda i, _: (weight_grads((t - 7) * 2 + i), 0)[1], 0)

        return 0

    lax.fori_loop(0, 6 + CAP, tick, 0)

    def drain(c, _):
        take(in_tiles.at[c, pl.ds(0, n_hold - 1)], e_send.at[c])
        take(rows.at[c, pl.ds(0, 3)], a_send.at[c])
        take(rows.at[c, pl.ds(0, 3)], f_send.at[c])
        take(rows.at[c, 0], h_send.at[c])
        take(tsend.at[c], t_send.at[c])
        take(r1s.at[c], r1_send.at[c])
        take(r2s.at[c], r2_send.at[c])
        take(fin.at[c, pl.ds(0, n_hold - 1)], b_send.at[c])
        return 0

    lax.fori_loop(0, CAP, drain, 0)


def write_out(grad_v, gw_in_v, gw_out_v, grad_h, gw_in_h, gw_out_h, sem):
    copies = [
        pltpu.make_async_copy(src, dst, sem.at[i])
        for i, (src, dst) in enumerate(((grad_v, grad_h), (gw_in_v, gw_in_h), (gw_out_v, gw_out_h)))
    ]
    for copy in copies:
        copy.start()
    for copy in copies:
        copy.wait()


def exchange_and_compute(route, inputs, grad_out, w_first, w_second):
    hid, feat = w_first.shape
    bf16, f32 = jnp.bfloat16, jnp.float32
    n_hold = NX * NZ
    vmem, anywhere = pl.BlockSpec(memory_space=pltpu.VMEM), pl.BlockSpec(memory_space=pl.ANY)
    hbm = pl.BlockSpec(memory_space=pltpu.HBM)
    dma = pltpu.SemaphoreType.DMA
    shapes = (
        jax.ShapeDtypeStruct((inputs.shape[0], feat), bf16),
        jax.ShapeDtypeStruct((hid, feat), bf16),
        jax.ShapeDtypeStruct((hid, feat), bf16),
    )
    made = pl.pallas_call(
        kernel,
        out_shape=shapes,
        in_specs=[vmem, hbm, hbm, hbm, hbm],
        out_specs=(vmem, vmem, vmem),
        scratch_shapes=[
            pltpu.VMEM(inputs.shape, bf16),
            pltpu.VMEM(inputs.shape, bf16),
            pltpu.VMEM((hid, feat), bf16),
            pltpu.VMEM((hid, feat), bf16),
            pltpu.VMEM((CAP, n_hold, 128), bf16),
            pltpu.VMEM((inputs.shape[0], feat), f32),
            pltpu.VMEM((CAP, n_hold, 2 * TILES, LANE), bf16),
            pltpu.VMEM((CAP, n_hold, 2 * TILES, LANE), bf16),
            pltpu.VMEM((CAP, 2 * NY, 32, 2 * feat), bf16),
            pltpu.VMEM((CAP, hid, 256), bf16),
            pltpu.VMEM((CAP, hid, 256), bf16),
            pltpu.VMEM((2, NY, 32, hid), bf16),
            pltpu.VMEM((n_hold, feat), bf16),
            pltpu.VMEM((CAP, NY, 32, feat), bf16),
            pltpu.VMEM((CAP, NY, 32, feat), bf16),
            pltpu.VMEM((4, NY, 32, feat), f32),
            pltpu.VMEM((CAP, 2, SUB, feat), bf16),
            pltpu.VMEM((CAP, 2, SUB, feat), bf16),
            pltpu.VMEM((CAP, 2, 32, feat), bf16),
            pltpu.VMEM((CAP, 2, 32, feat), bf16),
            pltpu.VMEM((CAP, n_hold, TILES, LANE), bf16),
            pltpu.VMEM((CAP, n_hold, TILES, LANE), bf16),
            dma((4,)),
            dma((CAP,)), dma((CAP,)),
            dma((CAP,)), dma((CAP,)), dma((CAP,)),
            dma((CAP, 4)), dma((CAP, 4)),
            dma((CAP,)), dma((CAP,)),
            dma((CAP,)), dma((CAP, 2)),
            dma((CAP,)), dma((CAP, 2)),
            dma((CAP,)), dma((CAP,)),
        ],
        compiler_params=pltpu.CompilerParams(
            collective_id=0, has_side_effects=True, vmem_limit_bytes=48 * 1024 * 1024
        ),
    )(route, inputs, grad_out, w_first, w_second)
    return pl.pallas_call(
        write_out,
        out_shape=shapes,
        in_specs=[vmem] * 3,
        out_specs=(anywhere,) * 3,
        scratch_shapes=[dma((3,))],
        compiler_params=pltpu.CompilerParams(vmem_limit_bytes=1024 * 1024),
    )(*made)


def body(inputs, grad_out, lang_ids, lang_block, block_owner, w_in, w_out):
    lang_row = jnp.pad(lang_block, (0, 256 - lang_block.shape[0]), constant_values=-1)
    owner_row = jnp.pad(block_owner, (0, 128 - block_owner.shape[0]), constant_values=-1)
    route = jnp.concatenate([lang_row, owner_row, lang_ids])[None]
    grad_in, g_in, g_out = exchange_and_compute(route, inputs, grad_out, w_in[0], w_out[0])
    return (grad_in, g_in[None], g_out[None])


def solution(mesh):
    in_specs = (
        P(("dp", "lang"), None),
        P(("dp", "lang"), None),
        P(("dp", "lang")),
        P(),
        P(),
        P("lang", "dp", None),
        P("lang", "dp", None),
    )
    out_specs = (P(("dp", "lang"), None), P("lang", "dp", None), P("lang", "dp", None))
    return jax.shard_map(body, mesh=mesh, in_specs=in_specs, out_specs=out_specs, check_vma=False)
```

time: 125 us -> 112 us (0.90)
  Pallas kernels: 115 us -> 108 us
  matrix products: 2.84 us -> 0 us
  local copies, waits for them, and re-layouts: 3.94 us -> 2.08 us
    pallas_call x1 -> x2, Pallas kernels: 115 us -> 108 us  [the longest x1 106 us: exchange_and_compute(): pl.pallas_call(kernel, out_shape=shapes, in_specs=[vmem, hbm, hbm, hbm, h...]
    dot_general x2 -> x0, matrix products: 2.84 us -> none  [the longest x1 1.69 us: body(): jnp.dot(onehot, packed, preferred_element_type=jnp.float32)]
    unnamed x5 -> x4, local copies, waits for them, and re-layouts: 3.94 us -> 2.08 us
    reduce_sum x3 -> x0, other arithmetic: 1.72 us -> none  [the longest x1 0.78 us: slots_of(): jnp.sum(jnp.where(lang_block[:, None] == jnp.arange(n_hold)[None, :], blo...]
where the time goes in v3:
time: 112 us
  Pallas kernels  108 us (96%)
  local copies, waits for them, and re-layouts  2.08 us (2%)
    pallas_call x1, Pallas kernels, exchange_and_compute(): pl.pallas_call(kernel, out_shape=shapes, in_specs=[vmem, hbm, hbm, hbm, h...  106 us

profile of v3, /device:TPU:32, one launch (start us, length us, event | category | flops | bytes accessed | tf_op | source)
XLA Modules:
  0.0 111.8 jit_solution(8629005226798353326)
XLA Ops:
  0.6 0.7 fusion
  1.3 0.0 copy-start
  1.3 1.0 copy-done
  2.4 0.0 copy-start.1
  2.4 1.0 copy-done.1
  3.4 106.2 %shard_map.94 = (bf16[128,2048]{1,0:T(8,128)(2,1)S(1)}, bf16[512,2048]{1,0:T(8,128)(2,1)S(1)}, bf16[512,2048]{1,0:T(8,128)(2,1)S(1)}) custom-call(s32[1,512]{1,0:T(1,128)S(1)} %bitcast.5, bf16[128,2048]{1,0:T(8,128)(2,1)S(1)} %copy-done, bf16[128,2048]{1,0:T(8,128)(2,1)S(1)} %copy-done.1, bf16[512,2048]{1,0:T(8,128)(2,1)} %bitcast.6, bf16[512,2048]{1,0:T(8,128)(2,1)} %bitcast.7), custom_call_target="tpu_custom_call" | custom-call | tf_op jit(solution)/shard_map/pallas_call | solution.py:350
  109.6 2.2 %shard_map.95 = (bf16[128,2048]{1,0:T(8,128)(2,1)}, bf16[512,2048]{1,0:T(8,128)(2,1)}, bf16[512,2048]{1,0:T(8,128)(2,1)}) custom-call(bf16[128,2048]{1,0:T(8,128)(2,1)S(1)} %get-tuple-element.9.grad_v, bf16[512,2048]{1,0:T(8,128)(2,1)S(1)} %get-tuple-element.10.gw_in_v, bf16[512,2048]{1,0:T(8,128)(2,1)S(1)} %get-tuple-element.11.gw_out_v), custom_call_target="tpu_custom_call" | custom-call | tf_op jit(solution)/shard_map/pallas_call | solution.py:391
Async XLA Ops:
  1.3 1.0 copy-start
  2.4 1.0 copy-start.1

commit v4 on v3

--- a/solution.py
+++ b/solution.py
@@ -27,21 +27,42 @@
     return (gelu_value, gelu_slope)
 
 
-def placement(route, swap_type):
+NEAR = (0, 4)
+FAR = (2, 3)
+LAST_SLOT = 1
+
+
+def offset_of(i, far):
+    return (i >> 2) & 3, (i & 3) - 1 + 4 * far
+
+
+def placement(route, x, z, kind):
     n_hold = NX * NZ
 
     def picks(shape, values):
         at = lax.broadcasted_iota(jnp.int32, shape, 0)
-        return jnp.where(at == values, 1.0, 0.0).astype(swap_type)
+        return jnp.where(at == values, 1.0, 0.0).astype(kind)
 
     lang_of_row = picks((256, 128), route[:, 384:512])
-    block_of_lang = dot_nn(picks((128, 256), route[:, 0:256]), lang_of_row).astype(swap_type)
+    block_of_lang = dot_nn(picks((128, 256), route[:, 0:256]), lang_of_row).astype(kind)
     holder = dot_nn(picks((n_hold, 128), route[:, 256:384]), block_of_lang)
     row = lax.broadcasted_iota(jnp.int32, (128, 128), 0)
     later = lax.broadcasted_iota(jnp.int32, (128, 128), 1)
-    before = jnp.where(row < later, 1.0, 0.0).astype(swap_type)
-    earlier = dot_nn(holder.astype(swap_type), before)
-    return [jnp.where(earlier == float(slot), holder, 0.0).astype(swap_type) for slot in range(CAP)]
+    earlier = dot_nn(holder.astype(kind), jnp.where(row < later, 1.0, 0.0).astype(kind))
+    index = lax.broadcasted_iota(jnp.int32, (n_hold, 128), 0)
+    holder_of_row = jnp.sum(holder * index.astype(jnp.float32), axis=0, keepdims=True)
+    count_of_row = jnp.sum(holder * earlier, axis=0, keepdims=True)
+    placed = []
+    for c in range(CAP):
+        if c == LAST_SLOT:
+            peer, far, slot = index & 15, index >> 4, jnp.full_like(index, CAP - 1)
+        else:
+            peer, far, slot = index >> 1, int(c not in NEAR), (index & 1) + (2 if c in (FAR[1], NEAR[1]) else 0)
+        dx, dz = offset_of(peer, far)
+        target = ((x + dx) & (NX - 1)) * NZ + ((z + dz + NZ) & (NZ - 1))
+        hit = (holder_of_row == target.astype(jnp.float32)) & (count_of_row == slot.astype(jnp.float32))
+        placed.append(jnp.where(hit, 1.0, 0.0).astype(kind))
+    return placed
 
 
 def dot_nt(a, b):
@@ -53,15 +74,16 @@
 
 
 def kernel(
-    route_ref, x_hbm, g_hbm, w_in_hbm, w_out_hbm,
+    route_ref, both_ref, w_in_hbm, w_out_hbm,
     grad_ref, gw_in_ref, gw_out_ref,
-    x_ref, g_ref, w_in, w_out, place, total_ref, out_tiles, in_tiles, rows, act_t, pg_t, pg, slots, tsend, trecv, own, r1s, r1r, r2s, r2r, fin, back,
+    w_in, w_out, place, total_ref, out_tiles, in_tiles, rows, act_t, pg_t, pg, slots, tsend, trecv, own, r1s, r1r, r2s, r2r, fin, back,
     w_sem, e_send, e_recv, a_send, f_send, h_send, y_recv, c_recv,
     t_send, t_recv, r1_send, r1_recv, r2_send, r2_recv, b_send, b_recv,
 ):
     dp, lang = lax.axis_index("dp"), lax.axis_index("lang")
     y, k = dp // 2, dp % 2
     n_hold = NX * NZ
+    x, z = lang // NZ, lang % NZ
     y_up, y_down, y_far = (y + 1) % NY, (y + NY - 1) % NY, (y + 2) % NY
     up, down, twin = (y_up * 2 + k, lang), (y_down * 2 + k, lang), (y * 2 + 1 - k, lang)
     d_up, d_down, d_far = y_up * 2 + k, y_down * 2 + k, y_far * 2 + k
@@ -77,11 +99,7 @@
         pltpu.make_async_copy(w_in_hbm, w_in, w_sem.at[0]),
         pltpu.make_async_copy(w_out_hbm, w_out, w_sem.at[1]),
     ]
-    row_copies = [
-        pltpu.make_async_copy(x_hbm, x_ref, w_sem.at[2]),
-        pltpu.make_async_copy(g_hbm, g_ref, w_sem.at[3]),
-    ]
-    for copy in (*row_copies, *w_copies):
+    for copy in w_copies:
         copy.start()
 
     barrier = pltpu.get_barrier_semaphore()
@@ -99,15 +117,15 @@
 
     feat = w_in.shape[1]
     hid = w_in.shape[0]
-    for slot, picked in enumerate(placement(route_ref[...], jnp.bfloat16)):
+    for slot, picked in enumerate(placement(route_ref[...], x, z, jnp.bfloat16)):
         place[slot] = picked
 
     def to_tiles(matrix, width):
         return jnp.concatenate([matrix[:, j * LANE : (j + 1) * LANE] for j in range(width)], axis=0)
 
     def dispatch(c):
-        x_rows = dot_nn(place[c], x_ref[...]).astype(jnp.bfloat16)
-        g_rows = dot_nn(place[c], g_ref[...]).astype(jnp.bfloat16)
+        picked = dot_nn(place[c], both_ref[...]).astype(jnp.bfloat16)
+        x_rows, g_rows = picked[:, :feat], picked[:, feat:]
         for g in range(2):
             at = slice(g * SUB, (g + 1) * SUB)
             both = jnp.concatenate([to_tiles(x_rows[at], TILES), to_tiles(g_rows[at], TILES)], axis=1)
@@ -115,15 +133,44 @@
             out_tiles[c, at, :TILES] = both[:, :LANE].reshape(SUB, TILES, LANE)
             out_tiles[c, at, TILES:] = both[:, LANE:].reshape(SUB, TILES, LANE)
 
+    x_at = [((x + d) % NX) * NZ for d in range(NX)]
+    z_at = [(z + d) % NZ for d in range(NZ)]
+
+    def exchange(c, src, dst, s_sem, r_sem, sign):
+        def one(i, at, far):
+            dx, dz = offset_of(i, far)
+            if dx == 0 and dz == 0:
+                pltpu.make_async_copy(src.at[c, at], dst.at[c, at], r_sem.at[c]).start()
+            else:
+                to = x_at[sign * dx % NX] + z_at[sign * dz % NZ]
+                send(src.at[c, at], dst.at[c, at], s_sem.at[c], r_sem.at[c], (dp, to))
+
+        far_first = (2, 1, 3, 0)
+        order = [4 * a + b for b in far_first for a in (2, 1, 3, 0)]
+
+        @pl.when((c == NEAR[0]) | (c == NEAR[1]))
+        def _():
+            for i in order:
+                one(i, pl.ds(2 * i, 2), 0)
+
+        @pl.when((c == FAR[0]) | (c == FAR[1]))
+        def _():
+            for i in order:
+                one(i, pl.ds(2 * i, 2), 1)
+
+        @pl.when(c == LAST_SLOT)
+        def _():
+            for far in (1, 0):
+                for i in order:
+                    one(i, pl.ds(far * 16 + i, 1), far)
+
+    def sent(c, ref, sem):
+        pl.when((c == NEAR[0]) | (c == NEAR[1]))(lambda: take(ref.at[c, pl.ds(0, n_hold - 2)], sem.at[c]))
+        pl.when(c == LAST_SLOT)(lambda: take(ref.at[c, pl.ds(0, n_hold - 1)], sem.at[c]))
+        pl.when((c == FAR[0]) | (c == FAR[1]))(lambda: take(ref.at[c], sem.at[c]))
+
     def start_exchange(c):
-        pltpu.make_async_copy(out_tiles.at[c, lang], in_tiles.at[c, lang], e_recv.at[c]).start()
-
-        def one(i, _):
-            to = (lang + i) % n_hold
-            send(out_tiles.at[c, to], in_tiles.at[c, lang], e_send.at[c], e_recv.at[c], (dp, to))
-            return 0
-
-        lax.fori_loop(1, n_hold, one, 0)
+        exchange(c, out_tiles, in_tiles, e_send, e_recv, 1)
 
     def start_next(c):
         @pl.when(c + 1 < CAP)
@@ -131,9 +178,9 @@
             start_exchange(c + 1)
 
     def prepare(c):
-        @pl.when(c + 2 < CAP)
-        def _():
-            dispatch(c + 2)
+        @pl.when(c + 3 < CAP)
+        def _():
+            dispatch(c + 3)
 
     def start_gather(c):
         take(in_tiles.at[c], e_recv.at[c])
@@ -169,35 +216,38 @@
             take(block, y_recv.at[c, 2 + i])
             send(block, block, h_send.at[c], c_recv.at[c, 3], twin)
 
-    def compute(c):
+    def hidden(c, f):
+        at = pl.ds(f * 256, 256)
+        x_rows = rows[c, :, :, :feat].reshape(2 * NY * 32, feat)
+        g_rows = rows[c, :, :, feat:].reshape(2 * NY * 32, feat)
+        value, slope = gelu_parts(dot_nt(w_in[at, :], x_rows))
+        pre_grad = (dot_nt(w_out[at, :], g_rows) * slope).astype(jnp.bfloat16)
+        act_t[c, at] = value.astype(jnp.bfloat16)
+        pg_t[c, at] = pre_grad
+        pre_grad = pre_grad.T
+        pre_grad = pre_grad.reshape(NY, 2, 32, 256)
+        for core in range(2):
+            pg[(core + k) % 2, :, :, at] = pre_grad[:, core]
+
+    def hidden_low(c):
         t_own, t_down = y * 2 + 1 - k, y_down * 2 + 1 - k
         t_up, t_far = y_up * 2 + 1 - k, y_far * 2 + 1 - k
         for i, d in enumerate((t_own, t_down, t_up, t_far)):
             take(rows.at[c, d], c_recv.at[c, i])
-
-        def hidden(f, _):
-            at = pl.ds(pl.multiple_of(f * 256, 256), 256)
-            x_rows = rows[c, :, :, :feat].reshape(2 * NY * 32, feat)
-            g_rows = rows[c, :, :, feat:].reshape(2 * NY * 32, feat)
-            value, slope = gelu_parts(dot_nt(x_rows, w_in[at, :]))
-            pre_grad = (dot_nt(g_rows, w_out[at, :]) * slope).astype(jnp.bfloat16)
-            act_t[c, at] = value.astype(jnp.bfloat16).T
-            pg_t[c, at] = pre_grad.T
-            pre_grad = pre_grad.reshape(NY, 2, 32, 256)
-            for core in range(2):
-                pg[(core + k) % 2, :, :, at] = pre_grad[:, core]
-            return 0
-
-        lax.fori_loop(0, hid // 256, hidden, 0)
-
-        def rows_grad(f, _):
+        hidden(c, 0)
+
+    def hidden_high(c):
+        hidden(c, 1)
+
+    def rows_grad(c):
+        def part_of(f, _):
             at = pl.ds(pl.multiple_of(f * 512, 512), 512)
             part = dot_nn(pg[...].reshape(2 * NY * 32, hid), w_in[:, at]).reshape(2, NY, 32, 512)
             own[c % 4, :, :, at] = part[0]
             tsend[c, :, :, at] = part[1].astype(jnp.bfloat16)
             return 0
 
-        lax.fori_loop(0, feat // 512, rows_grad, 0)
+        lax.fori_loop(0, feat // 512, part_of, 0)
         send(tsend.at[c], trecv.at[c], t_send.at[c], t_recv.at[c], twin)
 
     def reduce_far(c):
@@ -232,14 +282,7 @@
             total = total.astype(jnp.bfloat16)
             out = dot_nn(swap, to_tiles(total, TILES)).astype(jnp.bfloat16)
             fin[c, g * SUB : (g + 1) * SUB] = out.reshape(SUB, TILES, LANE)
-        pltpu.make_async_copy(fin.at[c, lang], back.at[c, lang], b_recv.at[c]).start()
-
-        def one(i, _):
-            to = (lang + i) % n_hold
-            send(fin.at[c, to], back.at[c, lang], b_send.at[c], b_recv.at[c], (dp, to))
-            return 0
-
-        lax.fori_loop(1, n_hold, one, 0)
+        exchange(c, fin, back, b_send, b_recv, -1)
 
     def finish(c):
         take(back.at[c], b_recv.at[c])
@@ -273,24 +316,30 @@
         gw_in_ref[:, at] = total_in.astype(jnp.bfloat16)
         gw_out_ref[:, at] = total_out.astype(jnp.bfloat16)
 
-    for copy in row_copies:
-        copy.wait()
     dispatch(0)
     pl.semaphore_wait(barrier, n_hold - 1 + 3)
     start_exchange(0)
     dispatch(1)
+    dispatch(2)
     total_ref[...] = jnp.zeros_like(total_ref)
 
+    def outputs(c):
+        weight_grads(2 * c)
+        weight_grads(2 * c + 1)
+
     stages = [
-        (0, start_gather),
-        (1, forward),
-        (0, prepare),
-        (2, compute),
-        (1, forward_far),
-        (3, reduce_far),
-        (4, reduce_near),
-        (5, reduce_last),
-        (6, finish),
+        (1, CAP, forward),
+        (0, CAP, start_gather),
+        (2, CAP, hidden_low),
+        (1, CAP, forward_far),
+        (2, CAP, hidden_high),
+        (3, CAP, reduce_far),
+        (2, CAP, rows_grad),
+        (4, CAP, reduce_near),
+        (0, CAP, prepare),
+        (5, CAP, reduce_last),
+        (7, 4, outputs),
+        (6, CAP, finish),
     ]
 
     def tick(t, _):
@@ -299,26 +348,22 @@
             for copy in w_copies:
                 copy.wait()
 
-        for offset, stage in stages:
-            pl.when((t >= offset) & (t < offset + CAP))(functools.partial(stage, t - offset))
-
-        @pl.when((t >= 7) & (t < 11))
-        def _():
-            lax.fori_loop(0, 2, lambda i, _: (weight_grads((t - 7) * 2 + i), 0)[1], 0)
+        for first, count, stage in stages:
+            pl.when((t >= first) & (t < first + count))(functools.partial(stage, t - first))
 
         return 0
 
-    lax.fori_loop(0, 6 + CAP, tick, 0)
+    lax.fori_loop(0, 11, tick, 0)
 
     def drain(c, _):
-        take(in_tiles.at[c, pl.ds(0, n_hold - 1)], e_send.at[c])
+        sent(c, in_tiles, e_send)
         take(rows.at[c, pl.ds(0, 3)], a_send.at[c])
         take(rows.at[c, pl.ds(0, 3)], f_send.at[c])
         take(rows.at[c, 0], h_send.at[c])
         take(tsend.at[c], t_send.at[c])
         take(r1s.at[c], r1_send.at[c])
         take(r2s.at[c], r2_send.at[c])
-        take(fin.at[c, pl.ds(0, n_hold - 1)], b_send.at[c])
+        sent(c, fin, b_send)
         return 0
 
     lax.fori_loop(0, CAP, drain, 0)
@@ -335,7 +380,7 @@
         copy.wait()
 
 
-def exchange_and_compute(route, inputs, grad_out, w_first, w_second):
+def exchange_and_compute(route, both, w_first, w_second):
     hid, feat = w_first.shape
     bf16, f32 = jnp.bfloat16, jnp.float32
     n_hold = NX * NZ
@@ -343,22 +388,20 @@
     hbm = pl.BlockSpec(memory_space=pltpu.HBM)
     dma = pltpu.SemaphoreType.DMA
     shapes = (
-        jax.ShapeDtypeStruct((inputs.shape[0], feat), bf16),
+        jax.ShapeDtypeStruct((both.shape[0], feat), bf16),
         jax.ShapeDtypeStruct((hid, feat), bf16),
         jax.ShapeDtypeStruct((hid, feat), bf16),
     )
     made = pl.pallas_call(
         kernel,
         out_shape=shapes,
-        in_specs=[vmem, hbm, hbm, hbm, hbm],
+        in_specs=[vmem, vmem, hbm, hbm],
         out_specs=(vmem, vmem, vmem),
         scratch_shapes=[
-            pltpu.VMEM(inputs.shape, bf16),
-            pltpu.VMEM(inputs.shape, bf16),
             pltpu.VMEM((hid, feat), bf16),
             pltpu.VMEM((hid, feat), bf16),
             pltpu.VMEM((CAP, n_hold, 128), bf16),
-            pltpu.VMEM((inputs.shape[0], feat), f32),
+            pltpu.VMEM((both.shape[0], feat), f32),
             pltpu.VMEM((CAP, n_hold, 2 * TILES, LANE), bf16),
             pltpu.VMEM((CAP, n_hold, 2 * TILES, LANE), bf16),
             pltpu.VMEM((CAP, 2 * NY, 32, 2 * feat), bf16),
@@ -375,7 +418,7 @@
             pltpu.VMEM((CAP, 2, 32, feat), bf16),
             pltpu.VMEM((CAP, n_hold, TILES, LANE), bf16),
             pltpu.VMEM((CAP, n_hold, TILES, LANE), bf16),
-            dma((4,)),
+            dma((2,)),
             dma((CAP,)), dma((CAP,)),
             dma((CAP,)), dma((CAP,)), dma((CAP,)),
             dma((CAP, 4)), dma((CAP, 4)),
@@ -387,7 +430,7 @@
         compiler_params=pltpu.CompilerParams(
             collective_id=0, has_side_effects=True, vmem_limit_bytes=48 * 1024 * 1024
         ),
-    )(route, inputs, grad_out, w_first, w_second)
+    )(route, both, w_first, w_second)
     return pl.pallas_call(
         write_out,
         out_shape=shapes,
@@ -402,7 +445,7 @@
     lang_row = jnp.pad(lang_block, (0, 256 - lang_block.shape[0]), constant_values=-1)
     owner_row = jnp.pad(block_owner, (0, 128 - block_owner.shape[0]), constant_values=-1)
     route = jnp.concatenate([lang_row, owner_row, lang_ids])[None]
-    grad_in, g_in, g_out = exchange_and_compute(route, inputs, grad_out, w_in[0], w_out[0])
+    grad_in, g_in, g_out = exchange_and_compute(route, jnp.concatenate([inputs, grad_out], axis=1), w_in[0], w_out[0])
     return (grad_in, g_in[None], g_out[None])
 
 

time: 112 us -> 106 us (0.946)
  Pallas kernels: 108 us -> 104 us
  local copies, waits for them, and re-layouts: 2.08 us -> 0 us
  other arithmetic: 0.7 us -> 1.98 us
    pallas_call x1, Pallas kernels: 106 us -> 102 us  [exchange_and_compute(): pl.pallas_call(kernel, out_shape=shapes, in_specs=[vmem, vmem, hbm, hbm],...]
    unnamed x4 -> x0, local copies, waits for them, and re-layouts: 2.08 us -> none
    concatenate x0 -> x1, other arithmetic: none -> 1.29 us  [body(): jnp.concatenate([inputs, grad_out], axis=1)]
where the time goes in v4:
time: 106 us
  Pallas kernels  104 us (98%)
  other arithmetic  1.98 us (2%)
    pallas_call x1, Pallas kernels, exchange_and_compute(): pl.pallas_call(kernel, out_shape=shapes, in_specs=[vmem, vmem, hbm, hbm],...  102 us
    pallas_call x1, Pallas kernels, exchange_and_compute(): pl.pallas_call(write_out, out_shape=shapes, in_specs=[vmem] * 3, out_spec...  2.21 us

profile of v4, /device:TPU:32, one launch (start us, length us, event | category | flops | bytes accessed | tf_op | source)
XLA Modules:
  0.0 106.4 jit_solution(13690571632693867571)
XLA Ops:
  0.6 0.7 fusion
  1.3 1.3 %pad_maximum_fusion.both_ref = bf16[128,4096]{1,0:T(8,128)(2,1)S(1)} fusion(bf16[128,2048]{1,0:T(8,128)(2,1)} %param.8, bf16[128,2048]{1,0:T(8,128)(2,1)} %param.7), kind=kLoop, calls=%fused_computation | loop fusion | flops 2097152 | bytes 2097152 | tf_op jit(solution)/shard_map/concatenate | solution.py:448
  2.6 101.5 %shard_map.94 = (bf16[128,2048]{1,0:T(8,128)(2,1)S(1)}, bf16[512,2048]{1,0:T(8,128)(2,1)S(1)}, bf16[512,2048]{1,0:T(8,128)(2,1)S(1)}) custom-call(s32[1,512]{1,0:T(1,128)S(1)} %bitcast.5, bf16[128,4096]{1,0:T(8,128)(2,1)S(1)} %pad_maximum_fusion.both_ref, bf16[512,2048]{1,0:T(8,128)(2,1)} %bitcast.6, bf16[512,2048]{1,0:T(8,128)(2,1)} %bitcast.7), custom_call_target="tpu_custom_call" | custom-call | tf_op jit(solution)/shard_map/pallas_call | solution.py:395
  104.1 2.2 %shard_map.95 = (bf16[128,2048]{1,0:T(8,128)(2,1)}, bf16[512,2048]{1,0:T(8,128)(2,1)}, bf16[512,2048]{1,0:T(8,128)(2,1)}) custom-call(bf16[128,2048]{1,0:T(8,128)(2,1)S(1)} %get-tuple-element.9.grad_v, bf16[512,2048]{1,0:T(8,128)(2,1)S(1)} %get-tuple-element.10.gw_in_v, bf16[512,2048]{1,0:T(8,128)(2,1)S(1)} %get-tuple-element.11.gw_out_v), custom_call_target="tpu_custom_call" | custom-call | tf_op jit(solution)/shard_map/pallas_call | solution.py:434

commit v5 on v4

--- a/solution.py
+++ b/solution.py
@@ -76,7 +76,7 @@
 def kernel(
     route_ref, both_ref, w_in_hbm, w_out_hbm,
     grad_ref, gw_in_ref, gw_out_ref,
-    w_in, w_out, place, total_ref, out_tiles, in_tiles, rows, act_t, pg_t, pg, slots, tsend, trecv, own, r1s, r1r, r2s, r2r, fin, back,
+    w_in, w_out, place, out_tiles, in_tiles, rows, act_t, pg_t, pg, slots, tsend, trecv, own, r1s, r1r, r2s, r2r, fin, back,
     w_sem, e_send, e_recv, a_send, f_send, h_send, y_recv, c_recv,
     t_send, t_recv, r1_send, r1_recv, r2_send, r2_recv, b_send, b_recv,
 ):
@@ -291,18 +291,20 @@
         for g in range(2):
             for j in range(TILES):
                 at = slice(g * LANE, (g + 1) * LANE)
-                slots[g * SUB : (g + 1) * SUB, j * LANE : (j + 1) * LANE] = flat[j * SUB : (j + 1) * SUB, at]
-
-        def add(f, _):
-            at = pl.ds(pl.multiple_of(f * 512, 512), 512)
-            part = lax.dot_general(
-                place[c], slots[:, at], (((0,), (0,)), ((), ())), preferred_element_type=jnp.float32
-            )
-            grad_ref[:, at] = (total_ref[:, at] + part).astype(jnp.bfloat16)
-            total_ref[:, at] = total_ref[:, at] + part
-            return 0
-
-        lax.fori_loop(0, feat // 512, add, 0)
+                slots[c, g * SUB : (g + 1) * SUB, j * LANE : (j + 1) * LANE] = flat[j * SUB : (j + 1) * SUB, at]
+
+        @pl.when(c == CAP - 1)
+        def _():
+            def combine(f, _):
+                at = pl.ds(pl.multiple_of(f * 512, 512), 512)
+                grad = lax.dot_general(
+                    place[...].reshape(CAP * n_hold, LANE), slots[:, :, at].reshape(CAP * n_hold, 512),
+                    (((0,), (0,)), ((), ())), preferred_element_type=jnp.float32,
+                )
+                grad_ref[:, at] = grad.astype(jnp.bfloat16)
+                return 0
+
+            lax.fori_loop(0, feat // 512, combine, 0)
 
     def weight_grads(f):
         at = pl.ds(pl.multiple_of(f * 256, 256), 256)
@@ -321,7 +323,6 @@
     start_exchange(0)
     dispatch(1)
     dispatch(2)
-    total_ref[...] = jnp.zeros_like(total_ref)
 
     def outputs(c):
         weight_grads(2 * c)
@@ -370,9 +371,13 @@
 
 
 def write_out(grad_v, gw_in_v, gw_out_v, grad_h, gw_in_h, gw_out_h, sem):
+    rows = grad_v.shape[0]
+    parts = [(grad_v, grad_h, 0)]
+    for first in range(0, gw_in_v.shape[0], rows):
+        parts += [(gw_in_v, gw_in_h, first), (gw_out_v, gw_out_h, first)]
     copies = [
-        pltpu.make_async_copy(src, dst, sem.at[i])
-        for i, (src, dst) in enumerate(((grad_v, grad_h), (gw_in_v, gw_in_h), (gw_out_v, gw_out_h)))
+        pltpu.make_async_copy(src.at[pl.ds(first, rows)], dst.at[pl.ds(first, rows)], sem.at[i])
+        for i, (src, dst, first) in enumerate(parts)
     ]
     for copy in copies:
         copy.start()
@@ -401,14 +406,13 @@
             pltpu.VMEM((hid, feat), bf16),
             pltpu.VMEM((hid, feat), bf16),
             pltpu.VMEM((CAP, n_hold, 128), bf16),
-            pltpu.VMEM((both.shape[0], feat), f32),
             pltpu.VMEM((CAP, n_hold, 2 * TILES, LANE), bf16),
             pltpu.VMEM((CAP, n_hold, 2 * TILES, LANE), bf16),
             pltpu.VMEM((CAP, 2 * NY, 32, 2 * feat), bf16),
             pltpu.VMEM((CAP, hid, 256), bf16),
             pltpu.VMEM((CAP, hid, 256), bf16),
             pltpu.VMEM((2, NY, 32, hid), bf16),
-            pltpu.VMEM((n_hold, feat), bf16),
+            pltpu.VMEM((CAP, n_hold, feat), bf16),
             pltpu.VMEM((CAP, NY, 32, feat), bf16),
             pltpu.VMEM((CAP, NY, 32, feat), bf16),
             pltpu.VMEM((4, NY, 32, feat), f32),
@@ -436,7 +440,7 @@
         out_shape=shapes,
         in_specs=[vmem] * 3,
         out_specs=(anywhere,) * 3,
-        scratch_shapes=[dma((3,))],
+        scratch_shapes=[dma((1 + 2 * hid // both.shape[0],))],
         compiler_params=pltpu.CompilerParams(vmem_limit_bytes=1024 * 1024),
     )(*made)
 

time: 106 us -> 105 us (level)
  Pallas kernels: 104 us -> 102 us
    pallas_call x1, Pallas kernels: 102 us -> 100 us  [exchange_and_compute(): pl.pallas_call(kernel, out_shape=shapes, in_specs=[vmem, vmem, hbm, hbm],...]
where the time goes in v5:
time: 105 us
  Pallas kernels  102 us (97%)
  other arithmetic  1.98 us (2%)
    pallas_call x1, Pallas kernels, exchange_and_compute(): pl.pallas_call(kernel, out_shape=shapes, in_specs=[vmem, vmem, hbm, hbm],...  100 us
    pallas_call x1, Pallas kernels, exchange_and_compute(): pl.pallas_call(write_out, out_shape=shapes, in_specs=[vmem] * 3, out_spec...  2.25 us

profile of v5, /device:TPU:32, one launch (start us, length us, event | category | flops | bytes accessed | tf_op | source)
XLA Modules:
  0.0 105.1 jit_solution(6333910094871047979)
XLA Ops:
  0.6 0.7 fusion
  1.3 1.3 %pad_maximum_fusion.both_ref = bf16[128,4096]{1,0:T(8,128)(2,1)S(1)} fusion(bf16[128,2048]{1,0:T(8,128)(2,1)} %param.8, bf16[128,2048]{1,0:T(8,128)(2,1)} %param.7), kind=kLoop, calls=%fused_computation | loop fusion | flops 2097152 | bytes 2097152 | tf_op jit(solution)/shard_map/concatenate | solution.py:452
  2.6 100.2 %shard_map.94 = (bf16[128,2048]{1,0:T(8,128)(2,1)S(1)}, bf16[512,2048]{1,0:T(8,128)(2,1)S(1)}, bf16[512,2048]{1,0:T(8,128)(2,1)S(1)}) custom-call(s32[1,512]{1,0:T(1,128)S(1)} %bitcast.5, bf16[128,4096]{1,0:T(8,128)(2,1)S(1)} %pad_maximum_fusion.both_ref, bf16[512,2048]{1,0:T(8,128)(2,1)} %bitcast.6, bf16[512,2048]{1,0:T(8,128)(2,1)} %bitcast.7), custom_call_target="tpu_custom_call" | custom-call | tf_op jit(solution)/shard_map/pallas_call | solution.py:400
  102.9 2.3 %shard_map.95 = (bf16[128,2048]{1,0:T(8,128)(2,1)}, bf16[512,2048]{1,0:T(8,128)(2,1)}, bf16[512,2048]{1,0:T(8,128)(2,1)}) custom-call(bf16[128,2048]{1,0:T(8,128)(2,1)S(1)} %get-tuple-element.9.grad_v, bf16[512,2048]{1,0:T(8,128)(2,1)S(1)} %get-tuple-element.10.gw_in_v, bf16[512,2048]{1,0:T(8,128)(2,1)S(1)} %get-tuple-element.11.gw_out_v), custom_call_target="tpu_custom_call" | custom-call | tf_op jit(solution)/shard_map/pallas_call | solution.py:438

commit v6 on v5

--- a/solution.py
+++ b/solution.py
@@ -324,8 +324,10 @@
     dispatch(1)
     dispatch(2)
 
-    def outputs(c):
+    def outputs_even(c):
         weight_grads(2 * c)
+
+    def outputs_odd(c):
         weight_grads(2 * c + 1)
 
     stages = [
@@ -338,8 +340,9 @@
         (2, CAP, rows_grad),
         (4, CAP, reduce_near),
         (0, CAP, prepare),
+        (7, 4, outputs_even),
         (5, CAP, reduce_last),
-        (7, 4, outputs),
+        (7, 4, outputs_odd),
         (6, CAP, finish),
     ]
 

time: 105 us -> 106 us (level); the launches traced: 105 us -> 105 us
  no operation moved by 1% of the time
where the time goes in v6:
time: 106 us; the launch traced here: 105 us
  Pallas kernels  102 us (96%)
  other arithmetic  1.98 us (2%)
    pallas_call x1, Pallas kernels, exchange_and_compute(): pl.pallas_call(kernel, out_shape=shapes, in_specs=[vmem, vmem, hbm, hbm],...  100 us
    pallas_call x1, Pallas kernels, exchange_and_compute(): pl.pallas_call(write_out, out_shape=shapes, in_specs=[vmem] * 3, out_spec...  2.25 us

profile of v6, /device:TPU:32, one launch (start us, length us, event | category | flops | bytes accessed | tf_op | source)
XLA Modules:
  0.0 105.0 jit_solution(13338234574140122293)
XLA Ops:
  0.6 0.7 fusion
  1.3 1.3 %pad_maximum_fusion.both_ref = bf16[128,4096]{1,0:T(8,128)(2,1)S(1)} fusion(bf16[128,2048]{1,0:T(8,128)(2,1)} %param.8, bf16[128,2048]{1,0:T(8,128)(2,1)} %param.7), kind=kLoop, calls=%fused_computation | loop fusion | flops 2097152 | bytes 2097152 | tf_op jit(solution)/shard_map/concatenate | solution.py:455
  2.6 100.1 %shard_map.94 = (bf16[128,2048]{1,0:T(8,128)(2,1)S(1)}, bf16[512,2048]{1,0:T(8,128)(2,1)S(1)}, bf16[512,2048]{1,0:T(8,128)(2,1)S(1)}) custom-call(s32[1,512]{1,0:T(1,128)S(1)} %bitcast.5, bf16[128,4096]{1,0:T(8,128)(2,1)S(1)} %pad_maximum_fusion.both_ref, bf16[512,2048]{1,0:T(8,128)(2,1)} %bitcast.6, bf16[512,2048]{1,0:T(8,128)(2,1)} %bitcast.7), custom_call_target="tpu_custom_call" | custom-call | tf_op jit(solution)/shard_map/pallas_call | solution.py:403
  102.7 2.3 %shard_map.95 = (bf16[128,2048]{1,0:T(8,128)(2,1)}, bf16[512,2048]{1,0:T(8,128)(2,1)}, bf16[512,2048]{1,0:T(8,128)(2,1)}) custom-call(bf16[128,2048]{1,0:T(8,128)(2,1)S(1)} %get-tuple-element.9.grad_v, bf16[512,2048]{1,0:T(8,128)(2,1)S(1)} %get-tuple-element.10.gw_in_v, bf16[512,2048]{1,0:T(8,128)(2,1)S(1)} %get-tuple-element.11.gw_out_v), custom_call_target="tpu_custom_call" | custom-call | tf_op jit(solution)/shard_map/pallas_call | solution.py:441
